TPU v7x, 128 devices: a whole 4x4x4 slice. The times are simulated.
128 devices in a mesh: tiles: 64 (over y_hi, z, x, core), chan: 2 (over y_lo).
Axes of the slice: x: 4, y: 4 (y_hi: 2, y_lo: 2; y = y_hi * 2 + y_lo), z: 4, core: 2. Of those that a mesh axis runs over, the one named last changes fastest.
Arguments:
- inputs: bfloat16 [64, 96, 96, 256], P('tiles', None, None, 'chan'), may hold values from -6 to 6
- cotangent: bfloat16 [64, 96, 96, 256], P('tiles', None, None, 'chan'), may hold values from -6 to 6
- wet: int32 [64, 96, 96], P('tiles'), may hold values from 0 to 1, as said below
- neighbours: int32 [64, 8], replicated, may hold values from -1 to 63, as said below
- depth_weight: float32 [7, 7, 256], P(None, None, 'chan'), may hold values from -0.875 to 0.875
- gamma: bfloat16 [256], P('chan'), may hold values from 0.5 to 1.5
- up_weight: bfloat16 [256, 1024], P(None, 'chan'), may hold values from -0.375 to 0.375
- up_bias: bfloat16 [1024], P('chan'), may hold values from -3 to 3
- down_weight: bfloat16 [1024, 256], P('chan'), may hold values from -0.1875 to 0.1875
- layer_scale: bfloat16 [256], P('chan'), may hold values from 0.29882812 to 1
Outputs:
- input_grad: bfloat16 [64, 96, 96, 256], P('tiles', None, None, 'chan')
- depth_weight_grad: float32 [7, 7, 256], P(None, None, 'chan')
- gamma_grad: float32 [256], P('chan')
- up_weight_grad: float32 [256, 1024], P(None, 'chan')
- up_bias_grad: float32 [1024], P('chan')
- down_weight_grad: float32 [1024, 256], P('chan')
- layer_scale_grad: float32 [256], P('chan')
Inputs may be any that keep to these rules, and one draw needn't show every extreme that they name: 1 on wet cells, 0 on land. `neighbours`: wet tiles are numbered in row order of a window of 24 x 4 tiles; entry d of tile t is the number of the wet tile beside t in direction d, or -1 where that tile is land or outside the window. Every listed neighbour is at most 5 numbers away from t, and some are exactly that far.
All inputs are finite; a program needn't handle non-finite values.
Results may differ from a plain program's by a relative error of at most 0.0095.
Values may be sent and summed in bfloat16 or wider, within the bound.
A program may use at most 320 MiB of HBM per device.

v0:
```python
import math

import jax
import jax.numpy as jnp
from jax import lax
from jax.sharding import PartitionSpec as P

KERNEL = 7
REACH = 5


root_half = 0.7071067811865476
density = 0.3989422804014327


def shifted(block, axis, distance):
    devices = range(lax.axis_size(axis))
    route = [(i - distance, i) for i in devices if i - distance in devices]
    return lax.ppermute(block, axis, route)


def gelu_pieces(hidden):
    normal_cdf = 0.5 * (1.0 + lax.erf(hidden * root_half))
    activated = hidden * normal_cdf
    slope = normal_cdf + hidden * jnp.exp(-0.5 * hidden * hidden) * density
    return (activated, slope)


def mlp_backward(normed, wet_grad, up_weight, down_weight, up_bias, layer_scale, grad_scale):
    hidden = jnp.dot(normed, up_weight, preferred_element_type=jnp.float32) + up_bias.astype(
        jnp.float32
    )
    activated, slope = gelu_pieces(hidden)
    activated = activated.astype(jnp.bfloat16)
    branch = jnp.dot(activated, down_weight, preferred_element_type=jnp.float32)
    scale_part = grad_scale * jnp.sum(wet_grad.astype(jnp.float32) * branch, 0)
    branch_grad = (wet_grad.astype(jnp.float32) * layer_scale.astype(jnp.float32)).astype(
        jnp.bfloat16
    )
    down_part = grad_scale * jnp.dot(activated.T, branch_grad, preferred_element_type=jnp.float32)
    hidden_grad = (
        jnp.dot(branch_grad, down_weight.T, preferred_element_type=jnp.float32) * slope
    ).astype(jnp.bfloat16)
    bias_part = grad_scale * jnp.sum(hidden_grad.astype(jnp.float32), 0)
    up_part = grad_scale * jnp.dot(normed.T, hidden_grad, preferred_element_type=jnp.float32)
    norm_grad = jnp.dot(hidden_grad, up_weight.T, preferred_element_type=jnp.float32)
    return (norm_grad, up_part, down_part, bias_part, scale_part)


def depth_forward(padded, weight):
    out_rows = padded.shape[0] - KERNEL + 1
    out_cols = padded.shape[1] - KERNEL + 1
    total = jnp.zeros((out_rows, out_cols, padded.shape[2]), jnp.float32)
    for row_off in range(KERNEL):
        for col_off in range(KERNEL):
            total = (
                total
                + padded[row_off : row_off + out_rows, col_off : col_off + out_cols].astype(
                    jnp.float32
                )
                * weight[row_off, col_off]
            )
    return total


def depth_backward(grad_padded, weight):
    out_rows = grad_padded.shape[0] - KERNEL + 1
    out_cols = grad_padded.shape[1] - KERNEL + 1
    total = jnp.zeros((out_rows, out_cols, grad_padded.shape[2]), jnp.float32)
    for row_off in range(KERNEL):
        for col_off in range(KERNEL):
            row_at = KERNEL - 1 - row_off
            col_at = KERNEL - 1 - col_off
            total = (
                total
                + grad_padded[row_at : row_at + out_rows, col_at : col_at + out_cols].astype(
                    jnp.float32
                )
                * weight[row_off, col_off]
            )
    return total


def filter_gradient(conv_grad, padded):
    out_rows = conv_grad.shape[0]
    out_cols = conv_grad.shape[1]
    grad_float = conv_grad.astype(jnp.float32)
    rows_out = []
    for row_off in range(KERNEL):
        entries = []
        for col_off in range(KERNEL):
            window = padded[row_off : row_off + out_rows, col_off : col_off + out_cols].astype(
                jnp.float32
            )
            entries.append(jnp.sum(grad_float * window, (0, 1)))
        rows_out.append(jnp.stack(entries))
    return jnp.stack(rows_out)


def neighbour_strips(strips, tile_links, my_index, fetch):
    edge_of = (1, 0, 3, 2, 1, 1, 0, 0)
    picked = [jnp.zeros_like(strips[0]) for direction in range(8)]
    for offset in range(-REACH, REACH + 1):
        if offset == 0:
            continue
        fetched = fetch(strips, offset)
        source = my_index - offset
        for direction in range(8):
            picked[direction] = jnp.where(
                tile_links[direction] == source, fetched[edge_of[direction]], picked[direction]
            )
    return picked


def surround(own, tile_links, my_index, fetch):
    margin = KERNEL // 2
    tile_side = own.shape[0]
    strips = jnp.stack(
        [
            own[:margin],
            own[tile_side - margin :],
            jnp.swapaxes(own[:, :margin], 0, 1),
            jnp.swapaxes(own[:, tile_side - margin :], 0, 1),
        ]
    )
    picked = neighbour_strips(strips, tile_links, my_index, fetch)
    north_side, south_side, west_side, east_side, north_west, north_east, south_west, south_east = (
        picked
    )
    upper = jnp.concatenate(
        [north_west[:, tile_side - margin :], north_side, north_east[:, :margin]], 1
    )
    middle = jnp.concatenate([jnp.swapaxes(west_side, 0, 1), own, jnp.swapaxes(east_side, 0, 1)], 1)
    lower = jnp.concatenate(
        [south_west[:, tile_side - margin :], south_side, south_east[:, :margin]], 1
    )
    return jnp.concatenate([upper, middle, lower], 0)


def body(
    inputs,
    cotangent,
    wet,
    neighbours,
    depth_weight,
    gamma,
    up_weight,
    up_bias,
    down_weight,
    layer_scale,
):
    tile_side = inputs.shape[1]
    half_chan = inputs.shape[3]
    tile_count = lax.axis_size("tiles")
    grad_scale = 1.0 / (tile_side * math.sqrt(tile_count))
    my_index = lax.axis_index("tiles")
    tile_links = lax.dynamic_index_in_dim(neighbours, my_index, 0, keepdims=False)
    wet_cells = wet[0].astype(jnp.bfloat16)[..., None]
    gamma_float = gamma.astype(jnp.float32)
    wet_input = inputs[0] * wet_cells
    wet_grad = cotangent[0] * wet_cells
    padded = surround(
        wet_input, tile_links, my_index, lambda strips, offset: shifted(strips, "tiles", offset)
    )
    padded, filtered = (padded, depth_forward(padded, depth_weight))
    all_chan = half_chan * lax.axis_size("chan")
    moment_sums = lax.psum((jnp.sum(filtered, -1), jnp.sum(filtered * filtered, -1)), "chan")
    average = moment_sums[0][..., None] / all_chan
    variance = moment_sums[1][..., None] / all_chan - average * average
    inv_spread = lax.rsqrt(variance + 1e-06)
    unit_norm = (filtered - average) * inv_spread
    normed = (unit_norm * gamma_float).astype(jnp.bfloat16)
    normed_full, grad_full, scale_full = (
        lax.all_gather(normed, "chan", axis=2, tiled=True),
        lax.all_gather(wet_grad, "chan", axis=2, tiled=True),
        lax.all_gather(layer_scale, "chan", axis=0, tiled=True),
    )
    norm_part, up_total, down_total, bias_total, scale_part = mlp_backward(
        normed_full.reshape(-1, all_chan),
        grad_full.reshape(-1, all_chan),
        up_weight,
        down_weight,
        up_bias,
        scale_full,
        grad_scale,
    )
    norm_grad, scale_total = (
        lax.psum_scatter(norm_part, "chan", scatter_dimension=1, tiled=True),
        lax.psum_scatter(scale_part, "chan", scatter_dimension=0, tiled=True),
    )
    norm_grad = norm_grad.reshape(tile_side, tile_side, half_chan)
    gain_total = grad_scale * jnp.sum(norm_grad * unit_norm, (0, 1))
    scaled_grad = norm_grad * gamma_float
    slope_sums = (
        lax.psum(jnp.sum(scaled_grad, -1).astype(jnp.bfloat16), "chan").astype(jnp.float32),
        lax.psum(jnp.sum(scaled_grad * unit_norm, -1).astype(jnp.bfloat16), "chan").astype(
            jnp.float32
        ),
    )
    conv_grad = (
        inv_spread
        * (
            scaled_grad
            - slope_sums[0][..., None] / all_chan
            - unit_norm * slope_sums[1][..., None] / all_chan
        )
    ).astype(jnp.bfloat16)
    grad_padded = surround(
        conv_grad, tile_links, my_index, lambda strips, offset: shifted(strips, "tiles", offset)
    )
    spread_back = depth_backward(grad_padded, depth_weight)
    filter_part = grad_scale * filter_gradient(conv_grad, padded)
    input_grad = (
        wet_grad.astype(jnp.float32) + wet_cells.astype(jnp.float32) * spread_back
    ).astype(jnp.bfloat16)
    input_grad, filter_part = (input_grad, filter_part)
    filter_total, gain_sum, up_sum, bias_sum, down_sum, scale_sum = lax.psum(
        (filter_part, gain_total, up_total, bias_total, down_total, scale_total), "tiles"
    )
    return (input_grad[None], filter_total, gain_sum, up_sum, bias_sum, down_sum, scale_sum)


def solution(mesh):
    return jax.shard_map(
        body,
        mesh=mesh,
        in_specs=(
            P("tiles", None, None, "chan"),
            P("tiles", None, None, "chan"),
            P("tiles", None, None),
            P(),
            P(None, None, "chan"),
            P("chan"),
            P(None, "chan"),
            P("chan"),
            P("chan", None),
            P("chan"),
        ),
        out_specs=(
            P("tiles", None, None, "chan"),
            P(None, None, "chan"),
            P("chan"),
            P(None, "chan"),
            P("chan"),
            P("chan", None),
            P("chan"),
        ),
        check_vma=False,
    )
```

profile of v0, /device:TPU:1, one launch (start us, length us, event | category | flops | bytes accessed | tf_op | source)
XLA Modules:
  0.0 1191.2 jit_solution(8325371353481624862)
XLA Ops:
  8.7 5.2 bitcast_multiply_fusion.1
  26.0 22.8 %collective-permute-done.9 = bf16[4,3,96,128]{3,1,2,0:T(4,128)(2,1)S(1)} collective-permute-done((bf16[4,3,96,128]{3,1,2,0:T(4,128)(2,1)}, bf16[4,3,96,128]{3,1,2,0:T(4,128)(2,1)S(1)}, u32[]{:S(2)}, u32[]{:S(2)}) %collective-permute-start.9) | collective-permute-done | bytes 294944 | tf_op jit(solution)/shard_map/ppermute | solution.py:19
  56.0 5.3 collective-permute-start.1
  125.2 5.4 maximum_maximum_fusion
  131.1 61.2 %multiply_reduce_fusion.3 = (f32[96,96]{1,0:T(8,128)}, f32[96,96]{1,0:T(8,128)}, f32[96,96,128]{2,1,0:T(8,128)}) fusion(f32[128]{0:T(128)S(1)} %get-tuple-element.145, bf16[99,102,128]{2,1,0:T(8,128)(2,1)} %get-tuple-element.87, f32[128]{0:T(128)S(1)} %get-tuple-element.146, f32[128]{0:T(128)S(1)} %get-tuple-element.99, f32[128]{0:T(128)S(1)} %get-tuple-element.100, ...), kind=kLoop, calls=%fused_computation.241 | loop fusion | flops 196982784 | bytes 106414592 | tf_op jit(solution)/shard_map/reduce_sum | solution.py:167
  193.2 38.3 %all-reduce.10.cloned.1.call-done = (f32[96,96]{1,0:T(8,128)}, f32[96,96]{1,0:T(8,128)}) async-done(((f32[96,96]{1,0:T(8,128)}, f32[96,96]{1,0:T(8,128)}), (f32[96,96]{1,0:T(8,128)}, f32[96,96]{1,0:T(8,128)})) %all-reduce.10.cloned.1.call-update) | async-done | bytes 73744 | tf_op jit(solution)/shard_map/psum | solution.py:167
  232.4 6.6 multiply_convert_fusion.2
  239.1 16.5 %all-gather = bf16[2,1,128]{2,1,0:T(2,128)(2,1)S(1)} all-gather(bf16[1,1,128]{2,1,0:T(2,128)(2,1)S(1)} %bitcast.317), channel_id=1, replica_groups=mesh['tiles'=64,'chan'=2] {'chan'}, dimensions={0}, use_global_device_ids=true | all-gather | bytes 768 | tf_op jit(solution)/shard_map/all_gather | solution.py:176
  255.5 44.8 %all-gather.4.cloned.1.call-done = bf16[96,96,256]{2,1,0:T(8,128)(2,1)} async-done(((bf16[96,96,128]{2,1,0:T(8,128)(2,1)}), bf16[96,96,256]{2,1,0:T(8,128)(2,1)}) %all-gather.4.cloned.1.call-update) | async-done | bytes 4718608 | tf_op jit(solution)/shard_map/all_gather | solution.py:175
  300.4 4.3 fusion.6
  304.7 63.5 %all-gather.6.cloned.1.call-done = bf16[96,96,256]{2,1,0:T(8,128)(2,1)} async-done(((bf16[96,96,128]{2,1,0:T(8,128)(2,1)}), bf16[96,96,256]{2,1,0:T(8,128)(2,1)}) %all-gather.6.cloned.1.call-update) | async-done | bytes 4718608 | tf_op jit(solution)/shard_map/all_gather | solution.py:174
  368.2 12.0 %multiply_convert_fusion = (bf16[9216,512]{1,0:T(8,128)(2,1)}, f32[9216,512]{1,0:T(8,128)}) fusion(f32[512]{0:T(512)S(1)} %convert_element_type.479, bf16[9216,256]{1,0:T(8,128)(2,1)} %bitcast.264, bf16[256,512]{1,0:T(8,128)(2,1)S(1)} %copy-done), kind=kOutput, calls=%fused_computation.57 | convolution fusion | flops 2444230656 | bytes 33294336 | tf_op jit(solution)/shard_map/dot_general | solution.py:30
  380.2 14.1 %convert_reduce_fusion = (f32[512]{0:T(512)S(1)}, bf16[9216,512]{1,0:T(8,128)(2,1)S(1)}) fusion(f32[9216,512]{1,0:T(8,128)} %get-tuple-element.160, f32[512]{0:T(512)S(1)} %convert_element_type.479, bf16[9216,256]{1,0:T(8,128)(2,1)S(1)} %copy-done.9, bf16[512,256]{1,0:T(8,128)(2,1)S(1)} %copy-done.102), kind=kOutput, calls=%fused_computation.58 | convolution fusion | flops 2477260288 | bytes 33296384 | tf_op jit(solution)/shard_map/dot_general | solution.py:42
  398.0 5.0 fusion.179
  405.0 7.9 fusion.138
  412.9 4.2 all-reduce
  417.2 8.5 convolution_multiply_fusion
  425.7 8.8 convolution_multiply_fusion.1
  434.5 82.9 %reduce-scatter.2.cloned.1.call-done = f32[9216,128]{1,0:T(8,128)} async-done(((f32[9216,256]{1,0:T(8,128)}), f32[9216,128]{1,0:T(8,128)}) %reduce-scatter.2.cloned.1.call-update) | async-done | bytes 4718608 | tf_op jit(solution)/shard_map/reduce_scatter | solution.py:188
  520.5 7.5 multiply_reduce_fusion
  528.0 5.8 all-reduce.4
  533.8 29.1 %fusion.128 = (f32[128]{0:T(128)S(1)}, f32[128]{0:T(128)S(1)}, f32[128]{0:T(128)S(1)}, f32[128]{0:T(128)S(1)}, f32[128]{0:T(128)S(1)}, /*index=5*/f32[128]{0:T(1...) fusion(bf16[99,102,128]{2,1,0:T(8,128)(2,1)} %get-tuple-element, ...), kind=kLoop, calls=%fused_computation.233 | loop fusion | flops 75495168 | bytes 54420992 | tf_op jit(solution)/shard_map/reduce_sum | solution.py:95
  563.0 7.5 fusion.127
  572.7 11.5 fusion.100
  590.9 4.2 collective-permute-start.15
  595.4 23.7 %collective-permute-done.19 = bf16[4,3,96,128]{3,1,2,0:T(4,128)(2,1)S(1)} collective-permute-done((bf16[4,3,96,128]{3,1,2,0:T(4,128)(2,1)}, bf16[4,3,96,128]{3,1,2,0:T(4,128)(2,1)S(1)}, u32[]{:S(2)}, u32[]{:S(2)}) %collective-permute-start.19) | collective-permute-done | bytes 294944 | tf_op jit(solution)/shard_map/ppermute | solution.py:19
  622.3 3.9 collective-permute-start.12
  626.3 6.2 collective-permute-start.11
  634.5 326.4 %all-reduce.1 = (f32[7,7,128]{2,1,0:T(8,128)}, f32[128]{0:T(128)}, f32[512]{0:T(512)}, f32[128]{0:T(128)}) all-reduce(f32[7,7,128]{2,1,0:T(8,128)S(1)} %broadcast_multiply_fusion.1, f32[128]{0:T(128)S(1)} %broadcast_multiply_fusion.4, f32[512]{0:T(512)S(1)} %broadcast_multiply_fusion.2, ...), channel_id=1, replica_groups=mesh['tiles'=64,'chan'=2] {'tiles'}, use_global_device_ids=true, to_apply=%region_58.59 | all-reduce | flops 7040 | bytes 56320 | tf_op jit(solution)/shard_map/psum | solution.py:217
  971.6 4.1 pad_maximum_fusion.1
  976.2 37.2 %fusion.137 = bf16[1,96,96,128]{3,2,1,0:T(8,128)(2,1)} fusion(f32[128]{0:T(128)S(1)} %copy-done.33, bf16[99,102,128]{2,1,0:T(8,128)(2,1)S(1)} %get-tuple-element.85, f32[128]{0:T(128)S(1)} %copy-done.35, f32[128]{0:T(128)S(1)} %copy-done.39, f32[128]{0:T(128)S(1)} %copy-done.41, f32[128]{0:T(128)S(1)} %copy-done.43, f32[128]{0:T(128)S(1)} %copy-done.45, ...), kind=kLoop, calls=%fused_computation.268 | loop fusion | flops 198180864 | bytes 106377728 | tf_op jit(solution)/shard_map/broadcast_in_dim | solution.py:220
  1013.4 167.2 %all-reduce.8.cloned.1.call-done = (f32[256,512]{1,0:T(8,128)}, f32[512,256]{1,0:T(8,128)}) async-done(((f32[256,512]{1,0:T(8,128)}, f32[512,256]{1,0:T(8,128)}), (f32[256,512]{1,0:T(8,128)}, f32[512,256]{1,0:T(8,128)})) %all-reduce.8.cloned.1.call-update) | async-done | bytes 1048592 | tf_op jit(solution)/shard_map/psum | solution.py:217
  (334 shorter events, 72.2 us)
Async XLA Ops:
  7.2 361.0 %copy-start = (bf16[256,512]{1,0:T(8,128)(2,1)S(1)}, bf16[256,512]{1,0:T(8,128)(2,1)}, u32[]{:S(2)}) copy-start(bf16[256,512]{1,0:T(8,128)(2,1)} %param.16) | copy-start | bytes 786436
  7.2 224.3 %all-reduce.10.cloned.1.call-start = ((), (), s32[]{:S(2)}) async-start(), calls=%async_computation.5 | async-start | bytes 196608 | tf_op jit(solution)/shard_map/psum | solution.py:167
  16.6 32.3 %collective-permute-start.9 = (bf16[4,3,96,128]{3,1,2,0:T(4,128)(2,1)}, bf16[4,3,96,128]{3,1,2,0:T(4,128)(2,1)S(1)}, u32[]{:S(2)}, u32[]{:S(2)}) collective-permute-start(bf16[4,3,96,128]{3,1,2,0:T(4,128)(2,1)} %pad_maximum_fusion.6), channel_id=1, source_target_pairs={{10,0},{12,2},{14,4},{16,6},{18,8},{20,10},{22,12},{24,14},{26,16}... | collective-permute-start | bytes 884744 | tf_op jit(solution)/shard_map/ppermute | solution.py:19
  17.8 32.9 %collective-permute-start.8 = (bf16[4,3,96,128]{3,1,2,0:T(4,128)(2,1)}, bf16[4,3,96,128]{3,1,2,0:T(4,128)(2,1)S(1)}, u32[]{:S(2)}, u32[]{:S(2)}) collective-permute-start(bf16[4,3,96,128]{3,1,2,0:T(4,128)(2,1)} %pad_maximum_fusion.6), channel_id=1, source_target_pairs={{8,0},{10,2},{12,4},{14,6},{16,8},{18,10},{20,12},{22,14},{24,16},... | collective-permute-start | bytes 884744 | tf_op jit(solution)/shard_map/ppermute | solution.py:19
  19.1 32.9 %collective-permute-start.7 = (bf16[4,3,96,128]{3,1,2,0:T(4,128)(2,1)}, bf16[4,3,96,128]{3,1,2,0:T(4,128)(2,1)S(1)}, u32[]{:S(2)}, u32[]{:S(2)}) collective-permute-start(bf16[4,3,96,128]{3,1,2,0:T(4,128)(2,1)} %pad_maximum_fusion.6), channel_id=1, source_target_pairs={{6,0},{8,2},{10,4},{12,6},{14,8},{16,10},{18,12},{20,14},{22,16},{... | collective-permute-start | bytes 884744 | tf_op jit(solution)/shard_map/ppermute | solution.py:19
  20.4 35.6 %collective-permute-start.6 = (bf16[4,3,96,128]{3,1,2,0:T(4,128)(2,1)}, bf16[4,3,96,128]{3,1,2,0:T(4,128)(2,1)S(1)}, u32[]{:S(2)}, u32[]{:S(2)}) collective-permute-start(bf16[4,3,96,128]{3,1,2,0:T(4,128)(2,1)} %pad_maximum_fusion.6), channel_id=1, source_target_pairs={{4,0},{6,2},{8,4},{10,6},{12,8},{14,10},{16,12},{18,14},{20,16},{2... | collective-permute-start | bytes 884744 | tf_op jit(solution)/shard_map/ppermute | solution.py:19
  21.7 39.6 %collective-permute-start.5 = (bf16[4,3,96,128]{3,1,2,0:T(4,128)(2,1)}, bf16[4,3,96,128]{3,1,2,0:T(4,128)(2,1)S(1)}, u32[]{:S(2)}, u32[]{:S(2)}) collective-permute-start(bf16[4,3,96,128]{3,1,2,0:T(4,128)(2,1)} %pad_maximum_fusion.6), channel_id=1, source_target_pairs={{2,0},{4,2},{6,4},{8,6},{10,8},{12,10},{14,12},{16,14},{18,16},{20... | collective-permute-start | bytes 884744 | tf_op jit(solution)/shard_map/ppermute | solution.py:19
  25.1 105.5 %copy-start.14 = (f32[128]{0:T(128)}, f32[128]{0:T(128)S(1)}, u32[]{:S(2)}) copy-start(f32[128]{0:T(128)S(1)} %get-tuple-element.136) | copy-start | bytes 1540
  25.1 105.5 %copy-start.16 = (f32[128]{0:T(128)}, f32[128]{0:T(128)S(1)}, u32[]{:S(2)}) copy-start(f32[128]{0:T(128)S(1)} %get-tuple-element.137) | copy-start | bytes 1540
  25.1 105.5 %copy-start.18 = (f32[128]{0:T(128)}, f32[128]{0:T(128)S(1)}, u32[]{:S(2)}) copy-start(f32[128]{0:T(128)S(1)} %get-tuple-element.138) | copy-start | bytes 1540
  25.1 105.5 %copy-start.20 = (f32[128]{0:T(128)}, f32[128]{0:T(128)S(1)}, u32[]{:S(2)}) copy-start(f32[128]{0:T(128)S(1)} %get-tuple-element.139) | copy-start | bytes 1540
  25.2 105.5 %copy-start.22 = (f32[128]{0:T(128)}, f32[128]{0:T(128)S(1)}, u32[]{:S(2)}) copy-start(f32[128]{0:T(128)S(1)} %get-tuple-element.140) | copy-start | bytes 1540
  48.8 66.2 %collective-permute-start.4 = (bf16[4,3,96,128]{3,1,2,0:T(4,128)(2,1)}, bf16[4,3,96,128]{3,1,2,0:T(4,128)(2,1)S(1)}, u32[]{:S(2)}, u32[]{:S(2)}) collective-permute-start(bf16[4,3,96,128]{3,1,2,0:T(4,128)(2,1)} %pad_maximum_fusion.6), channel_id=1, source_target_pairs={{0,2},{2,4},{4,6},{6,8},{8,10},{10,12},{12,14},{14,16},{16,18},{18... | collective-permute-start | bytes 884744 | tf_op jit(solution)/shard_map/ppermute | solution.py:19
  50.7 64.3 %collective-permute-start.3 = (bf16[4,3,96,128]{3,1,2,0:T(4,128)(2,1)}, bf16[4,3,96,128]{3,1,2,0:T(4,128)(2,1)S(1)}, u32[]{:S(2)}, u32[]{:S(2)}) collective-permute-start(bf16[4,3,96,128]{3,1,2,0:T(4,128)(2,1)} %pad_maximum_fusion.6), channel_id=1, source_target_pairs={{0,4},{2,6},{4,8},{6,10},{8,12},{10,14},{12,16},{14,18},{16,20},{1... | collective-permute-start | bytes 884744 | tf_op jit(solution)/shard_map/ppermute | solution.py:19
  52.1 63.0 %collective-permute-start.2 = (bf16[4,3,96,128]{3,1,2,0:T(4,128)(2,1)}, bf16[4,3,96,128]{3,1,2,0:T(4,128)(2,1)S(1)}, u32[]{:S(2)}, u32[]{:S(2)}) collective-permute-start(bf16[4,3,96,128]{3,1,2,0:T(4,128)(2,1)} %pad_maximum_fusion.6), channel_id=1, source_target_pairs={{0,6},{2,8},{4,10},{6,12},{8,14},{10,16},{12,18},{14,20},{16,22},{... | collective-permute-start | bytes 884744 | tf_op jit(solution)/shard_map/ppermute | solution.py:19
  56.0 59.0 %collective-permute-start.1 = (bf16[4,3,96,128]{3,1,2,0:T(4,128)(2,1)}, bf16[4,3,96,128]{3,1,2,0:T(4,128)(2,1)}, u32[]{:S(2)}, u32[]{:S(2)}) collective-permute-start(bf16[4,3,96,128]{3,1,2,0:T(4,128)(2,1)} %pad_maximum_fusion.6), channel_id=1, source_target_pairs={{0,8},{2,10},{4,12},{6,14},{8,16},{10,18},{12,20},{14,22},{16,24},... | collective-permute-start | bytes 884744 | tf_op jit(solution)/shard_map/ppermute | solution.py:19
  61.3 53.7 %collective-permute-start = (bf16[4,3,96,128]{3,1,2,0:T(4,128)(2,1)}, bf16[4,3,96,128]{3,1,2,0:T(4,128)(2,1)}, u32[]{:S(2)}, u32[]{:S(2)}) collective-permute-start(bf16[4,3,96,128]{3,1,2,0:T(4,128)(2,1)} %pad_maximum_fusion.6), channel_id=1, source_target_pairs={{0,10},{2,12},{4,14},{6,16},{8,18},{10,20},{12,22},{14,24},{16,26}... | collective-permute-start | bytes 884744 | tf_op jit(solution)/shard_map/ppermute | solution.py:19
  192.4 108.0 %all-gather.4.cloned.1.call-start = ((), (), s32[]{:S(2)}) async-start(), calls=%async_computation.1 | async-start | bytes 7077888 | tf_op jit(solution)/shard_map/all_gather | solution.py:175
  193.1 175.0 %all-gather.6.cloned.1.call-start = ((), (), s32[]{:S(2)}) async-start(), calls=%async_computation.2 | async-start | bytes 7077888 | tf_op jit(solution)/shard_map/all_gather | solution.py:174
  239.0 278.4 %reduce-scatter.2.cloned.1.call-start = ((), (), s32[]{:S(2)}) async-start(), calls=%async_computation.3 | async-start | bytes 14155776 | tf_op jit(solution)/shard_map/reduce_scatter | solution.py:188
  403.1 777.4 %all-reduce.8.cloned.1.call-start = ((), (), s32[]{:S(2)}) async-start(), calls=%async_computation.4 | async-start | bytes 2097152 | tf_op jit(solution)/shard_map/psum | solution.py:217
  585.5 33.6 %collective-permute-start.19 = (bf16[4,3,96,128]{3,1,2,0:T(4,128)(2,1)}, bf16[4,3,96,128]{3,1,2,0:T(4,128)(2,1)S(1)}, u32[]{:S(2)}, u32[]{:S(2)}) collective-permute-start(bf16[4,3,96,128]{3,1,2,0:T(4,128)(2,1)} %pad_maximum_fusion.7), channel_id=1, source_target_pairs={{10,0},{12,2},{14,4},{16,6},{18,8},{20,10},{22,12},{24,14},{26,16}... | collective-permute-start | bytes 884744 | tf_op jit(solution)/shard_map/ppermute | solution.py:19
  586.8 34.2 %collective-permute-start.18 = (bf16[4,3,96,128]{3,1,2,0:T(4,128)(2,1)}, bf16[4,3,96,128]{3,1,2,0:T(4,128)(2,1)S(1)}, u32[]{:S(2)}, u32[]{:S(2)}) collective-permute-start(bf16[4,3,96,128]{3,1,2,0:T(4,128)(2,1)} %pad_maximum_fusion.7), channel_id=1, source_target_pairs={{8,0},{10,2},{12,4},{14,6},{16,8},{18,10},{20,12},{22,14},{24,16},... | collective-permute-start | bytes 884744 | tf_op jit(solution)/shard_map/ppermute | solution.py:19
  588.3 34.0 %collective-permute-start.17 = (bf16[4,3,96,128]{3,1,2,0:T(4,128)(2,1)}, bf16[4,3,96,128]{3,1,2,0:T(4,128)(2,1)S(1)}, u32[]{:S(2)}, u32[]{:S(2)}) collective-permute-start(bf16[4,3,96,128]{3,1,2,0:T(4,128)(2,1)} %pad_maximum_fusion.7), channel_id=1, source_target_pairs={{6,0},{8,2},{10,4},{12,6},{14,8},{16,10},{18,12},{20,14},{22,16},{... | collective-permute-start | bytes 884744 | tf_op jit(solution)/shard_map/ppermute | solution.py:19
  589.6 36.7 %collective-permute-start.16 = (bf16[4,3,96,128]{3,1,2,0:T(4,128)(2,1)}, bf16[4,3,96,128]{3,1,2,0:T(4,128)(2,1)S(1)}, u32[]{:S(2)}, u32[]{:S(2)}) collective-permute-start(bf16[4,3,96,128]{3,1,2,0:T(4,128)(2,1)} %pad_maximum_fusion.7), channel_id=1, source_target_pairs={{4,0},{6,2},{8,4},{10,6},{12,8},{14,10},{16,12},{18,14},{20,16},{2... | collective-permute-start | bytes 884744 | tf_op jit(solution)/shard_map/ppermute | solution.py:19
  590.9 41.6 %collective-permute-start.15 = (bf16[4,3,96,128]{3,1,2,0:T(4,128)(2,1)}, bf16[4,3,96,128]{3,1,2,0:T(4,128)(2,1)S(1)}, u32[]{:S(2)}, u32[]{:S(2)}) collective-permute-start(bf16[4,3,96,128]{3,1,2,0:T(4,128)(2,1)} %pad_maximum_fusion.7), channel_id=1, source_target_pairs={{2,0},{4,2},{6,4},{8,6},{10,8},{12,10},{14,12},{16,14},{18,16},{20... | collective-permute-start | bytes 884744 | tf_op jit(solution)/shard_map/ppermute | solution.py:19
  619.1 341.8 %collective-permute-start.14 = (bf16[4,3,96,128]{3,1,2,0:T(4,128)(2,1)}, bf16[4,3,96,128]{3,1,2,0:T(4,128)(2,1)S(1)}, u32[]{:S(2)}, u32[]{:S(2)}) collective-permute-start(bf16[4,3,96,128]{3,1,2,0:T(4,128)(2,1)} %pad_maximum_fusion.7), channel_id=1, source_target_pairs={{0,2},{2,4},{4,6},{6,8},{8,10},{10,12},{12,14},{14,16},{16,18},{18... | collective-permute-start | bytes 884744 | tf_op jit(solution)/shard_map/ppermute | solution.py:19
  621.0 339.9 %collective-permute-start.13 = (bf16[4,3,96,128]{3,1,2,0:T(4,128)(2,1)}, bf16[4,3,96,128]{3,1,2,0:T(4,128)(2,1)S(1)}, u32[]{:S(2)}, u32[]{:S(2)}) collective-permute-start(bf16[4,3,96,128]{3,1,2,0:T(4,128)(2,1)} %pad_maximum_fusion.7), channel_id=1, source_target_pairs={{0,4},{2,6},{4,8},{6,10},{8,12},{10,14},{12,16},{14,18},{16,20},{1... | collective-permute-start | bytes 884744 | tf_op jit(solution)/shard_map/ppermute | solution.py:19
  622.3 338.6 %collective-permute-start.12 = (bf16[4,3,96,128]{3,1,2,0:T(4,128)(2,1)}, bf16[4,3,96,128]{3,1,2,0:T(4,128)(2,1)S(1)}, u32[]{:S(2)}, u32[]{:S(2)}) collective-permute-start(bf16[4,3,96,128]{3,1,2,0:T(4,128)(2,1)} %pad_maximum_fusion.7), channel_id=1, source_target_pairs={{0,6},{2,8},{4,10},{6,12},{8,14},{10,16},{12,18},{14,20},{16,22},{... | collective-permute-start | bytes 884744 | tf_op jit(solution)/shard_map/ppermute | solution.py:19
  626.3 334.6 %collective-permute-start.11 = (bf16[4,3,96,128]{3,1,2,0:T(4,128)(2,1)}, bf16[4,3,96,128]{3,1,2,0:T(4,128)(2,1)}, u32[]{:S(2)}, u32[]{:S(2)}) collective-permute-start(bf16[4,3,96,128]{3,1,2,0:T(4,128)(2,1)} %pad_maximum_fusion.7), channel_id=1, source_target_pairs={{0,8},{2,10},{4,12},{6,14},{8,16},{10,18},{12,20},{14,22},{16,24},... | collective-permute-start | bytes 884744 | tf_op jit(solution)/shard_map/ppermute | solution.py:19
  632.5 328.5 %collective-permute-start.10 = (bf16[4,3,96,128]{3,1,2,0:T(4,128)(2,1)}, bf16[4,3,96,128]{3,1,2,0:T(4,128)(2,1)}, u32[]{:S(2)}, u32[]{:S(2)}) collective-permute-start(bf16[4,3,96,128]{3,1,2,0:T(4,128)(2,1)} %pad_maximum_fusion.7), channel_id=1, source_target_pairs={{0,10},{2,12},{4,14},{6,16},{8,18},{10,20},{12,22},{14,24},{16,26}... | collective-permute-start | bytes 884744 | tf_op jit(solution)/shard_map/ppermute | solution.py:19
  976.1 208.1 %copy-start.1 = (bf16[256,512]{1,0:T(8,128)(2,1)S(1)}, bf16[256,512]{1,0:T(8,128)(2,1)}, u32[]{:S(2)}) copy-start(bf16[256,512]{1,0:T(8,128)(2,1)} %param.16) | copy-start | bytes 786436
  (99 other events, 1788.8 us)
Sparse Core Ops, SparseCore 0:
  192.5 38.9 all-reduce.9
  233.7 66.5 all-gather.3
  302.0 66.1 all-gather.5
  403.2 114.1 reduce-scatter.1
  520.3 660.1 all-reduce.7
where the time goes:
time: 1200 us; the launch traced here: 1190 us
  waiting for transfers between devices  444 us (37%)
  blocking collectives  353 us (29%)
  other arithmetic  209 us (17%)
  between operations  67.2 us (6%)
  matrix products  56.4 us (5%)
  starting transfers between devices  48.2 us (4%)
  local copies, waits for them, and re-layouts  13.8 us (1%)
    psum x1, blocking collectives, body(): lax.psum((filter_part, gain_total, up_total, bias_total, down_total, scal...  326 us
    psum x1, waiting for transfers between devices, body(): lax.psum((filter_part, gain_total, up_total, bias_total, down_total, scal...  167 us
    reduce_scatter x1, waiting for transfers between devices, body(): lax.psum_scatter(norm_part, 'chan', scatter_dimension=1, tiled=True)  82.9 us
    all_gather x1, waiting for transfers between devices, body(): lax.all_gather(normed, 'chan', axis=2, tiled=True)  63.5 us
    reduce_sum x1, other arithmetic, body(): jnp.sum(filtered * filtered, -1)  61.2 us
    reduce_sum x4, other arithmetic, filter_gradient(): entries.append(jnp.sum(grad_float * window, (0, 1)))  50.3 us
    ppermute x20, starting transfers between devices, shifted(): return lax.ppermute(block, axis, route)  48 us
    ppermute x20, waiting for transfers between devices, shifted(): return lax.ppermute(block, axis, route)  46.5 us
  transfers between devices with their start and end apart: 25, of which 7 were waited for; matrix products, arithmetic and copies ran while one was open for 13% of the time, Pallas kernels for 0%

commit v1 on v0

v1 whole, which is shorter than its diff:
```python
import functools
import math

import jax
import jax.numpy as jnp
from jax import lax
from jax.experimental import pallas as pl
from jax.experimental.pallas import tpu as pltpu
from jax.sharding import PartitionSpec as P

KERNEL = 7
MARGIN = 3
LANES = 128
CHAN = 256
HIDDEN = 1024
HALF_HIDDEN = 512
BLOCK = 256
ROWS = 8
COLS = 2
MLP_ROWS = 8
REACH = 5
F32 = jnp.float32
BF16 = jnp.bfloat16
MESH = pl.DeviceIdType.MESH
density = 0.3989422804014327


def gelu_pieces(hidden):
    size = jnp.abs(hidden)
    denom = 1.0 + 0.2316419 * size
    inverse = pl.reciprocal(denom, approx=True)
    inverse = inverse * (2.0 - denom * inverse)
    bell = jnp.exp(-0.5 * hidden * hidden)
    poly = 0.5 * 1.061405429
    for factor in (-1.453152027, 1.421413741, -0.284496736, 0.254829592):
        poly = poly * inverse + 0.5 * factor
    tail = poly * inverse * bell
    normal_cdf = jnp.where(hidden >= 0.0, 1.0 - tail, tail)
    activated = hidden * normal_cdf
    slope = normal_cdf + hidden * bell * density
    return activated, slope


def nn(a, b):
    return lax.dot_general(a, b, (((1,), (0,)), ((), ())), preferred_element_type=F32)


def nt(a, b):
    return lax.dot_general(a, b, (((1,), (1,)), ((), ())), preferred_element_type=F32)


def kernel(
    side, shape4,
    links, x_ref, c_ref, mask_ref, depth_ref, gamma_ref, up_ref, bias_ref, down_ref, scale_ref,
    out_ref, mats_ref, small_ref,
    pf, pg, taps, taps_acc, strips, corners, rows_in, cols_in, corners_in,
    wu, wd, pars, pars_in,
    grad_own, grad_send, grad_in, y_own, y_send, y_in, conv_send, conv_in,
    sums, gamma_acc, bias_acc, ring_core, ring_a, ring_b, ring_y, total,
    small_a, small_peer, small_peer_in, small_core, small_x, small_z, small_y,
    halo_send, halo_recv, weight_sem, weight_recv, grad_sem, grad_recv, y_sem, y_recv, conv_sem, conv_recv,
    rs_send, rs_recv, ag_send, ag_recv, sm_send, sm_recv,
):
    n_yh, n_z, n_x, n_core = shape4
    tiles = n_yh * n_z * n_x * n_core
    half = side // 2
    width = side + 16
    cells = half * side
    steps = half // MLP_ROWS
    chunk = MLP_ROWS * side
    me = lax.axis_index("tiles")
    h = lax.axis_index("chan")
    other = 1 - h
    core = me % n_core
    at_x = (me // n_core) % n_x
    at_z = (me // (n_core * n_x)) % n_z
    at_yh = me // (n_core * n_x * n_z)
    q = 1.0 / (side * math.sqrt(tiles))

    def tile_at(yh, z, x, c):
        return ((yh * n_z + z) * n_x + x) * n_core + c

    def dev(tile, chan=None):
        return {"tiles": tile, "chan": h if chan is None else chan}

    def remote(src, dst, send, recv, device):
        return pltpu.make_async_remote_copy(
            src_ref=src, dst_ref=dst, send_sem=send, recv_sem=recv, device_id=device, device_id_type=MESH
        )

    first = core * at_z + (1 - core) * at_x
    second = core * at_x + (1 - core) * at_z

    def ring_tile(a, b):
        return tile_at(at_yh, core * a + (1 - core) * b, core * b + (1 - core) * a, core)

    peer = dev(me, other)
    core_peer = dev(tile_at(at_yh, at_z, at_x, 1 - core))
    halo = [(sign, d) for sign in (1, -1) for d in range(1, REACH + 1)]

    def halo_tile(sign, d):
        return (me + sign * d + tiles) % tiles

    a_peers = [(first + k) % n_x for k in range(1, n_x)]
    b_peers = [(second + k) % n_x for k in range(1, n_x)]
    y_peers = [(0, 1), (1, 0), (1, 1)]

    def y_dev(dy, dc):
        return dev(tile_at((at_yh + dy) % 2, at_z, at_x, core), (h + dc) % 2)

    barrier = pltpu.get_barrier_semaphore()
    targets = [dev(halo_tile(s, d)) for s, d in halo]
    targets += [core_peer]
    targets += [dev(ring_tile(a, second)) for a in a_peers]
    targets += [dev(ring_tile(first, b)) for b in b_peers]
    targets += [y_dev(dy, dc) for dy, dc in y_peers]
    for target in targets:
        pl.semaphore_signal(barrier, inc=1, device_id=target, device_id_type=MESH)
    pl.semaphore_wait(barrier, len(targets))

    pars[...] = jnp.zeros_like(pars)
    pars[0:1, :] = bias_ref[...].astype(F32)
    pars[1:2, 0:LANES] = gamma_ref[...].astype(F32)
    pars[2:3, 0:LANES] = scale_ref[...].astype(F32)
    weight_copies = [
        remote(pars, pars_in, weight_sem.at[0], weight_recv.at[0], peer),
        remote(up_ref, wu.at[h], weight_sem.at[1], weight_recv.at[1], peer),
        remote(down_ref, wd.at[h], weight_sem.at[2], weight_recv.at[2], peer),
    ]
    weight_arrivals = [
        remote(pars, pars_in, weight_sem.at[0], weight_recv.at[0], peer),
        remote(up_ref, wu.at[other], weight_sem.at[1], weight_recv.at[1], peer),
        remote(down_ref, wd.at[other], weight_sem.at[2], weight_recv.at[2], peer),
    ]
    for copy in weight_copies:
        copy.start()

    def fill_input(i, _):
        at = pl.multiple_of(i * side, side)
        to = pl.multiple_of((i + MARGIN) * width + 8, 8)
        pf[pl.ds(to, side), :] = (x_ref[pl.ds(at, side), :] * mask_ref[pl.ds(at, side), :]).astype(F32)
        return 0

    lax.fori_loop(0, side, fill_input, 0)

    def make_strips(padded):
        for side_at, row in enumerate((MARGIN, side)):
            for k in range(MARGIN):
                base = (row + k) * width + 8
                strips[side_at, k * side : (k + 1) * side, :] = padded[base : base + side, :].astype(BF16)
                near = base if side_at == 0 else base + side - 16
                corners[side_at, k * 16 : (k + 1) * 16, :] = padded[near : near + 16, :].astype(BF16)
        for side_at, col in enumerate((8, 8 + side - MARGIN)):
            for k in range(MARGIN):
                line = padded[pl.ds(MARGIN * width + col + k, side, stride=width), :]
                strips[2 + side_at, k * side : (k + 1) * side, :] = line.astype(BF16)

    def halo_copies(phase):
        copies = []
        for n, (sign, d) in enumerate(halo):
            device = dev(halo_tile(sign, d))
            way = 0 if sign > 0 else 1
            send = halo_send.at[phase, n]
            recv = halo_recv.at[phase, n]
            if d < REACH:
                copies.append(remote(strips.at[1 - way], rows_in.at[phase, way, d - 1], send, recv, device))
            else:
                copies.append(remote(corners.at[1 - way], corners_in.at[phase, way], send, recv, device))
        for way, sign in enumerate((1, -1)):
            device = dev(halo_tile(sign, 1))
            n = len(halo) + way
            copies.append(
                remote(strips.at[3 - way], cols_in.at[phase, way], halo_send.at[phase, n], halo_recv.at[phase, n], device)
            )
        return copies

    def match(direction, source):
        return jnp.logical_and(links[me, direction] == source, source >= 0).astype(F32)

    def fill_halo(padded, phase):
        for way, sign in enumerate((-1, 1)):
            straight, left, right, beside = ((0, 4, 5, 2), (1, 6, 7, 3))[way]
            row = 0 if way == 0 else side + MARGIN
            straight_hit = [match(straight, me + sign * d) for d in range(1, 5)]
            left_hit = [match(left, me + sign * d) for d in range(1, 6)]
            right_hit = [match(right, me + sign * d) for d in range(1, 6)]
            far_hit = left_hit[4] if way == 0 else right_hit[4]
            for k in range(MARGIN):
                base = (row + k) * width
                lines = [rows_in[phase, way, d, k * side : (k + 1) * side, :].astype(F32) for d in range(4)]
                far = corners_in[phase, way, k * 16 : (k + 1) * 16, :].astype(F32)
                middle = sum(hit * line for hit, line in zip(straight_hit, lines))
                west = sum(hit * line[side - 8 :] for hit, line in zip(left_hit[:4], lines))
                east = sum(hit * line[:8] for hit, line in zip(right_hit[:4], lines))
                if way == 0:
                    west = west + far_hit * far[8:]
                else:
                    east = east + far_hit * far[:8]
                padded[base : base + 8, :] = west
                padded[base + 8 : base + 8 + side, :] = middle
                padded[base + 8 + side : base + 16 + side, :] = east
            hit = match(beside, me + sign)
            col = 8 - MARGIN if way == 0 else 8 + side
            for k in range(MARGIN):
                line = cols_in[phase, way, k * side : (k + 1) * side, :].astype(F32)
                padded[pl.ds(MARGIN * width + col + k, side, stride=width), :] = line * hit

    make_strips(pf)
    forward_halo = halo_copies(0)
    for copy in forward_halo:
        copy.start()

    def grad_copy(k):
        at = pl.ds(pl.multiple_of(k * chunk, chunk), chunk)
        return remote(grad_send.at[at, :], grad_in.at[at, :], grad_sem.at[k], grad_recv.at[k], peer)

    def fill_grad(k, _):
        there = pl.ds(pl.multiple_of(other * cells + k * chunk, chunk), chunk)
        here = pl.ds(pl.multiple_of(h * cells + k * chunk, chunk), chunk)
        at = pl.ds(pl.multiple_of(k * chunk, chunk), chunk)
        grad_send[at, :] = c_ref[there, :] * mask_ref[there, :]
        grad_copy(k).start()
        grad_own[at, :] = c_ref[here, :] * mask_ref[here, :]
        return 0

    lax.fori_loop(0, steps, fill_grad, 0)

    for a in range(KERNEL):
        for b in range(KERNEL):
            n = (a * KERNEL + b) * 8
            taps[n : n + 8, :] = jnp.broadcast_to(depth_ref[a, b : b + 1, :], (8, LANES))

    for copy in forward_halo:
        copy.wait_recv()
    fill_halo(pf, 0)

    def conv_block(padded, row, col, flip):
        base = row * width + col + 8 - MARGIN
        acc = [[None] * COLS for _ in range(ROWS)]
        for b in range(KERNEL):
            weights = []
            for a in range(KERNEL):
                n = a * KERNEL + b
                n = (KERNEL * KERNEL - 1 - n if flip else n) * 8
                weights.append(taps[n : n + 8, :])
            for r in range(ROWS + KERNEL - 1):
                for v in range(COLS):
                    value = padded[pl.ds(base + (r * width + v * 8 + b), 8), :]
                    for a in range(KERNEL):
                        i = r - a
                        if 0 <= i < ROWS:
                            term = value * weights[a]
                            acc[i][v] = term if acc[i][v] is None else acc[i][v] + term
        return acc

    col_steps = side // (8 * COLS)

    def conv_rows(start, put):
        def one(c, _):
            col = pl.multiple_of(c * (8 * COLS), 8 * COLS)
            acc = conv_block(pf, start, col, False)
            for i in range(ROWS):
                put(i, col, jnp.concatenate(acc[i], 0))
            return 0

        lax.fori_loop(0, col_steps, one, 0)

    def y_copy(k):
        at = pl.ds(pl.multiple_of(k * chunk, chunk), chunk)
        return remote(y_send.at[at, :], y_in.at[at, :], y_sem.at[k], y_recv.at[k], peer)

    def conv_there(k, _):
        def put(i, col, value):
            at = pl.multiple_of((k * ROWS + i) * side + col, 8 * COLS)
            y_send[pl.ds(at, 8 * COLS), :] = value.astype(BF16)

        conv_rows(other * half + k * ROWS, put)
        y_copy(k).start()
        return 0

    lax.fori_loop(0, steps, conv_there, 0)

    def conv_here(k, _):
        def put(i, col, value):
            at = pl.multiple_of((k * ROWS + i) * side + col, 8 * COLS)
            y_own[pl.ds(at, 8 * COLS), :] = value.astype(BF16)

        conv_rows(h * half + k * ROWS, put)
        return 0

    lax.fori_loop(0, steps, conv_here, 0)

    for copy in weight_arrivals:
        copy.wait_recv()
    wu[h] = up_ref[...]
    wd[h] = down_ref[...]
    mine = h == 0

    def ordered(own, others):
        return jnp.where(mine, own, others), jnp.where(mine, others, own)

    def row_of(n):
        own, others = pars[n : n + 1, 0:LANES], pars_in[n : n + 1, 0:LANES]
        return jnp.concatenate(ordered(own, others), 1)

    gamma_row = row_of(1)
    scale_row = row_of(2)
    bias_rows = ordered(pars[0:1, :], pars_in[0:1, :])

    sums[...] = jnp.zeros_like(sums)
    gamma_acc[...] = jnp.zeros_like(gamma_acc)
    bias_acc[...] = jnp.zeros_like(bias_acc)

    def conv_copy(k):
        at = pl.ds(pl.multiple_of(k * chunk, chunk), chunk)
        return remote(conv_send.at[at, :], conv_in.at[at, :], conv_sem.at[k], conv_recv.at[k], peer)

    def mlp(k, _):
        at = pl.ds(pl.multiple_of(k * chunk, chunk), chunk)
        y_copy(k).wait_recv()
        grad_copy(k).wait_recv()
        low, high = ordered(y_own[at, :].astype(F32), y_in[at, :].astype(F32))
        y = jnp.concatenate((low, high), 1)
        centred = y - jnp.sum(y, 1, keepdims=True) * (1.0 / CHAN)
        spread = jnp.sum(centred * centred, 1, keepdims=True) * (1.0 / CHAN)
        inv_spread = lax.rsqrt(spread + 1e-06)
        unit = centred * inv_spread
        normed = (unit * gamma_row).astype(BF16)
        low, high = ordered(grad_own[at, :].astype(F32), grad_in[at, :].astype(F32))
        branch_grad = (jnp.concatenate((low, high), 1) * scale_row).astype(BF16)
        branch_t = branch_grad.T
        normed_t = normed.T
        norm_grad = jnp.zeros((chunk, CHAN), F32)
        for block in range(HIDDEN // BLOCK):
            slot, off = divmod(block * BLOCK, HALF_HIDDEN)
            w_up = wu[slot, :, off : off + BLOCK]
            w_down = wd[slot, off : off + BLOCK, :]
            cols = slice(block * BLOCK, (block + 1) * BLOCK)
            hidden = nn(normed, w_up) + bias_rows[slot][:, off : off + BLOCK]
            activated, slope = gelu_pieces(hidden)
            hidden_grad = (nt(branch_grad, w_down) * slope).astype(BF16)
            sums[1, :, cols] += nn(branch_t, activated.astype(BF16))
            sums[0, :, cols] += nn(normed_t, hidden_grad)
            bias_acc[:, cols] += jnp.sum(hidden_grad.astype(F32).reshape(chunk // 8, 8, BLOCK), 0)
            norm_grad = norm_grad + nt(hidden_grad, w_up)
        gamma_acc[...] += jnp.sum((norm_grad * unit).reshape(chunk // 8, 8, CHAN), 0)
        scaled = norm_grad * gamma_row
        mean = jnp.sum(scaled, 1, keepdims=True) * (1.0 / CHAN)
        tilt = jnp.sum(scaled * unit, 1, keepdims=True) * (1.0 / CHAN)
        conv_grad = (inv_spread * (scaled - mean - unit * tilt)).astype(BF16).astype(F32)
        own, away = ordered(conv_grad[:, :LANES], conv_grad[:, LANES:])
        conv_send[at, :] = away.astype(BF16)
        conv_copy(k).start()
        for i in range(MLP_ROWS):
            to = pl.multiple_of((MARGIN + h * half + k * MLP_ROWS + i) * width + 8, 8)
            pg[pl.ds(to, side), :] = own[i * side : (i + 1) * side]
        return 0

    lax.fori_loop(0, steps, mlp, 0)

    rs_core = remote(sums.at[1 - core], ring_core, rs_send.at[0], rs_recv.at[0], core_peer)
    rs_core.start()

    ident = lax.broadcasted_iota(jnp.int32, (CHAN, CHAN), 0) == lax.broadcasted_iota(jnp.int32, (CHAN, CHAN), 1)
    down_sums = sums[1]
    down_high = down_sums.astype(BF16)
    down_low = (down_sums - down_high.astype(F32)).astype(BF16)
    paired = jnp.zeros((CHAN, CHAN), F32)
    for slot in range(2):
        cols = slice(slot * HALF_HIDDEN, (slot + 1) * HALF_HIDDEN)
        paired = paired + nn(down_high[:, cols], wd[slot]) + nn(down_low[:, cols], wd[slot])
    scale_sum = jnp.sum(jnp.where(ident, paired, 0.0), 0, keepdims=True) / scale_row
    gamma_sum = jnp.sum(gamma_acc[...], 0, keepdims=True)
    bias_sum = jnp.sum(bias_acc[...], 0, keepdims=True)
    small_peer[...] = jnp.zeros_like(small_peer)
    small_a[...] = jnp.zeros_like(small_a)
    n_taps = KERNEL * KERNEL

    def put_small(ref, at, value, n):
        own, away = ordered(value[:, : n * LANES], value[:, n * LANES :])
        for i in range(n):
            ref[0][ref[1] + at + i : ref[1] + at + i + 1, :] = own[:, i * LANES : (i + 1) * LANES]
            small_peer[at + i : at + i + 1, :] = away[:, i * LANES : (i + 1) * LANES]

    place = (small_a, n_taps)
    put_small(place, 0, gamma_sum, 1)
    put_small(place, 1, scale_sum, 1)
    put_small(place, 2, bias_sum, 4)
    small_chan = remote(small_peer, small_peer_in, sm_send.at[0], sm_recv.at[0], peer)
    small_chan.start()

    def take_conv(k, _):
        conv_copy(k).wait_recv()
        for i in range(MLP_ROWS):
            at = pl.multiple_of((k * MLP_ROWS + i) * side, side)
            to = pl.multiple_of((MARGIN + other * half + k * MLP_ROWS + i) * width + 8, 8)
            pg[pl.ds(to, side), :] = conv_in[pl.ds(at, side), :].astype(F32)
        return 0

    lax.fori_loop(0, steps, take_conv, 0)
    for copy in forward_halo:
        copy.wait_send()
    make_strips(pg)
    backward_halo = halo_copies(1)
    for copy in backward_halo:
        copy.start()

    rs_core.wait_recv()
    sums[core] = sums[core] + ring_core[...]
    a_rows, b_rows, y_rows = CHAN // n_x, CHAN // n_x // n_z, CHAN // n_x // n_z // 2
    rs_a = []
    for k, a in enumerate(a_peers):
        piece = sums.at[core, pl.ds(pl.multiple_of(a * a_rows, a_rows), a_rows), :]
        rs_a.append(remote(piece, ring_a.at[k], rs_send.at[1 + k], rs_recv.at[1 + k], dev(ring_tile(a, second))))
    for copy in rs_a:
        copy.start()

    taps_acc[...] = jnp.zeros_like(taps_acc)

    def filter_block(n, _):
        row = (n // col_steps) * ROWS
        col = (n % col_steps) * (8 * COLS)
        inner = (row + MARGIN) * width + col + 8
        base = row * width + col + 8 - MARGIN
        grads = [
            [pg[pl.ds(pl.multiple_of(inner, 8) + (i * width + v * 8), 8), :] for v in range(COLS)] for i in range(ROWS)
        ]
        for b in range(KERNEL):
            acc = [None] * KERNEL
            for r in range(ROWS + KERNEL - 1):
                for v in range(COLS):
                    value = pf[pl.ds(base + (r * width + v * 8 + b), 8), :]
                    for a in range(KERNEL):
                        i = r - a
                        if 0 <= i < ROWS:
                            term = value * grads[i][v]
                            acc[a] = term if acc[a] is None else acc[a] + term
            for a in range(KERNEL):
                n = (a * KERNEL + b) * 8
                taps_acc[n : n + 8, :] += acc[a]
        return 0

    blocks = (side // ROWS) * col_steps
    lax.fori_loop(0, blocks // 2, filter_block, 0)

    for copy in rs_a:
        copy.wait_recv()
    a_at = pl.ds(pl.multiple_of(first * a_rows, a_rows), a_rows)
    sums[core, a_at, :] = sums[core, a_at, :] + sum(ring_a[k] for k in range(n_x - 1))
    rs_b = []
    for k, b in enumerate(b_peers):
        piece = sums.at[core, pl.ds(pl.multiple_of(first * a_rows + b * b_rows, b_rows), b_rows), :]
        rs_b.append(remote(piece, ring_b.at[k], rs_send.at[4 + k], rs_recv.at[4 + k], dev(ring_tile(first, b))))
    for copy in rs_b:
        copy.start()

    lax.fori_loop(blocks // 2, blocks, filter_block, 0)

    for copy in rs_b:
        copy.wait_recv()
    b_start = first * a_rows + second * b_rows
    b_at = pl.ds(pl.multiple_of(b_start, b_rows), b_rows)
    sums[core, b_at, :] = sums[core, b_at, :] + sum(ring_b[k] for k in range(n_x - 1))

    def y_piece(yh, chan):
        rows = pl.ds(pl.multiple_of(b_start + yh * y_rows, y_rows), y_rows)
        return (core, rows, pl.ds(pl.multiple_of(chan * HALF_HIDDEN, HALF_HIDDEN), HALF_HIDDEN))

    rs_y = []
    for k, (dy, dc) in enumerate(y_peers):
        piece = sums.at[y_piece((at_yh + dy) % 2, (h + dc) % 2)]
        rs_y.append(remote(piece, ring_y.at[k], rs_send.at[7 + k], rs_recv.at[7 + k], y_dev(dy, dc)))
    for copy in rs_y:
        copy.start()

    for n in range(n_taps):
        small_a[n : n + 1, :] = jnp.sum(taps_acc[n * 8 : n * 8 + 8, :], 0, keepdims=True)
    small_chan.wait_recv()
    for n in range(6):
        small_a[n_taps + n : n_taps + n + 1, :] += small_peer_in[n : n + 1, :]
    sm_core = remote(small_a, small_core, sm_send.at[1], sm_recv.at[1], core_peer)
    sm_core.start()

    for copy in backward_halo:
        copy.wait_recv()
    fill_halo(pg, 1)

    def input_rows(k, _):
        row = k * ROWS

        def one(c, _):
            col = pl.multiple_of(c * (8 * COLS), 8 * COLS)
            acc = conv_block(pg, row, col, True)
            for i in range(ROWS):
                at = pl.ds(pl.multiple_of((row + i) * side + col, 8 * COLS), 8 * COLS)
                wet = mask_ref[at, :].astype(F32)
                grad = c_ref[at, :].astype(F32)
                out_ref[at, :] = (wet * (grad + jnp.concatenate(acc[i], 0))).astype(BF16)
            return 0

        lax.fori_loop(0, col_steps, one, 0)
        return 0

    row_steps = side // ROWS
    marks = [row_steps * n // 4 for n in range(5)]
    lax.fori_loop(marks[0], marks[1], input_rows, 0)

    for copy in rs_y:
        copy.wait_recv()
    y_start = b_start + at_yh * y_rows
    y_at = pl.ds(pl.multiple_of(y_start, y_rows), y_rows)
    total[core, y_at, :] = sums[y_piece(at_yh, h)] + (ring_y[0] + ring_y[1] + ring_y[2])
    y_mate = dev(tile_at((at_yh + 1) % 2, at_z, at_x, core))
    ag_y = remote(total.at[core, y_at, :], total.at[core, y_at, :], ag_send.at[0], ag_recv.at[0], y_mate)
    ag_y.start()
    sm_core.wait_recv()

    def small_stage(ref, value, at, size, base, tile):
        ref[at] = value
        copies = []
        for k in range(1, size):
            there = (at + k) % size
            copies.append(
                remote(ref.at[at], ref.at[at], sm_send.at[base + k - 1], sm_recv.at[base + k - 1], dev(tile(there)))
            )
        for copy in copies:
            copy.start()
        return copies

    sm_x = small_stage(
        small_x, small_a[...] + small_core[...], at_x, n_x, 2, lambda x: tile_at(at_yh, at_z, x, core)
    )
    lax.fori_loop(marks[1], marks[2], input_rows, 0)

    ag_y.wait_recv()
    ag_b = []
    for k, b in enumerate(b_peers):
        block = total.at[core, b_at, :]
        ag_b.append(remote(block, block, ag_send.at[1 + k], ag_recv.at[1 + k], dev(ring_tile(first, b))))
    for copy in ag_b:
        copy.start()
    for copy in sm_x:
        copy.wait_recv()
    sm_z = small_stage(
        small_z, sum(small_x[k] for k in range(n_x)), at_z, n_z, 5, lambda z: tile_at(at_yh, z, at_x, core)
    )
    lax.fori_loop(marks[2], marks[3], input_rows, 0)

    for copy in ag_b:
        copy.wait_recv()
    ag_a = []
    for k, a in enumerate(a_peers):
        block = total.at[core, a_at, :]
        ag_a.append(remote(block, block, ag_send.at[4 + k], ag_recv.at[4 + k], dev(ring_tile(a, second))))
    for copy in ag_a:
        copy.start()
    for copy in sm_z:
        copy.wait_recv()
    sm_y = small_stage(
        small_y, sum(small_z[k] for k in range(n_z)), at_yh, 2, 8, lambda yh: tile_at(yh, at_z, at_x, core)
    )
    lax.fori_loop(marks[3], marks[4], input_rows, 0)

    for copy in ag_a:
        copy.wait_recv()
    ag_core = remote(total.at[core], total.at[core], ag_send.at[7], ag_recv.at[7], core_peer)
    ag_core.start()
    for copy in sm_y:
        copy.wait_recv()
    small_ref[...] = (small_y[0] + small_y[1]) * q
    mats_ref[core] = total[core] * q
    ag_core.wait_recv()
    mats_ref[1 - core] = total[1 - core] * q

    for copy in weight_copies + backward_halo + [rs_core, small_chan, sm_core, ag_y, ag_core]:
        copy.wait_send()
    for copy in rs_a + rs_b + rs_y + ag_a + ag_b + sm_x + sm_z + sm_y:
        copy.wait_send()

    def finish(k, _):
        grad_copy(k).wait_send()
        y_copy(k).wait_send()
        conv_copy(k).wait_send()
        return 0

    lax.fori_loop(0, steps, finish, 0)


SHAPES = {64: (2, 4, 4, 2), 16: (2, 2, 2, 2)}


def block_call(inputs, cotangent, mask, neighbours, depth_weight, gamma, up_weight, up_bias, down_weight, layer_scale):
    side = inputs.shape[1]
    half_chan = inputs.shape[3]
    flat = (side * side, half_chan)
    shape4 = SHAPES[lax.axis_size("tiles")]
    n_yh, n_z, n_x, n_core = shape4
    width = side + 16
    cells = side * side // 2
    steps = side // 2 // MLP_ROWS
    a_rows = CHAN // n_x
    vmem, smem = pltpu.VMEM, pl.BlockSpec(memory_space=pltpu.SMEM)
    whole = pl.BlockSpec(memory_space=pltpu.VMEM)
    dma = pltpu.SemaphoreType.DMA
    padded = vmem(((side + 2 * MARGIN) * width, LANES), F32)
    taps = vmem((KERNEL * KERNEL * 8, LANES), F32)
    piece = vmem((cells, LANES), BF16)
    small = vmem((64, LANES), F32)
    pars = vmem((8, HALF_HIDDEN), F32)
    scratch = [
        padded, padded, taps, taps,
        vmem((4, MARGIN * side, LANES), BF16),
        vmem((2, MARGIN * 16, LANES), BF16),
        vmem((2, 2, 4, MARGIN * side, LANES), BF16),
        vmem((2, 2, MARGIN * side, LANES), BF16),
        vmem((2, 2, MARGIN * 16, LANES), BF16),
        vmem((2, CHAN, HALF_HIDDEN), BF16),
        vmem((2, HALF_HIDDEN, CHAN), BF16),
        pars, pars,
        piece, piece, piece, piece, piece, piece, piece, piece,
        vmem((2, CHAN, HIDDEN), F32),
        vmem((8, CHAN), F32),
        vmem((8, HIDDEN), F32),
        vmem((CHAN, HIDDEN), F32),
        vmem((n_x - 1, a_rows, HIDDEN), F32),
        vmem((n_x - 1, a_rows // n_z, HIDDEN), F32),
        vmem((3, a_rows // n_z // 2, HALF_HIDDEN), F32),
        vmem((2, CHAN, HALF_HIDDEN), F32),
        small, vmem((8, LANES), F32), vmem((8, LANES), F32), small,
        vmem((n_x, 64, LANES), F32), vmem((n_z, 64, LANES), F32), vmem((2, 64, LANES), F32),
        dma((2, 12)), dma((2, 12)), dma((3,)), dma((3,)),
        dma((steps,)), dma((steps,)), dma((steps,)), dma((steps,)), dma((steps,)), dma((steps,)),
        dma((10,)), dma((10,)), dma((8,)), dma((8,)), dma((9,)), dma((9,)),
    ]
    return pl.pallas_call(
        functools.partial(kernel, side, shape4),
        out_shape=(
            jax.ShapeDtypeStruct(flat, BF16),
            jax.ShapeDtypeStruct((2, CHAN, HALF_HIDDEN), F32),
            jax.ShapeDtypeStruct((64, LANES), F32),
        ),
        in_specs=[smem] + [whole] * 9,
        out_specs=(whole, whole, whole),
        scratch_shapes=scratch,
        compiler_params=pltpu.CompilerParams(
            collective_id=0, has_side_effects=True, vmem_limit_bytes=60 * 1024 * 1024
        ),
    )(
        neighbours,
        inputs.reshape(flat),
        cotangent.reshape(flat),
        mask,
        depth_weight,
        gamma.reshape(1, half_chan),
        up_weight,
        up_bias.reshape(1, -1),
        down_weight,
        layer_scale.reshape(1, half_chan),
    )


def body(
    inputs,
    cotangent,
    wet,
    neighbours,
    depth_weight,
    gamma,
    up_weight,
    up_bias,
    down_weight,
    layer_scale,
):
    side = inputs.shape[1]
    mask = jnp.broadcast_to(wet[0].astype(BF16)[..., None], (side, side, LANES)).reshape(side * side, LANES)
    grad, mats, small = block_call(
        inputs, cotangent, mask, neighbours, depth_weight, gamma, up_weight, up_bias, down_weight, layer_scale
    )
    taps = KERNEL * KERNEL
    return (
        grad.reshape(inputs.shape),
        small[:taps].reshape(KERNEL, KERNEL, LANES),
        small[taps],
        mats[0],
        small[taps + 2 : taps + 6].reshape(-1),
        mats[1].T,
        small[taps + 1],
    )


def solution(mesh):
    return jax.shard_map(
        body,
        mesh=mesh,
        in_specs=(
            P("tiles", None, None, "chan"),
            P("tiles", None, None, "chan"),
            P("tiles", None, None),
            P(),
            P(None, None, "chan"),
            P("chan"),
            P(None, "chan"),
            P("chan"),
            P("chan", None),
            P("chan"),
        ),
        out_specs=(
            P("tiles", None, None, "chan"),
            P(None, None, "chan"),
            P("chan"),
            P(None, "chan"),
            P("chan"),
            P("chan", None),
            P("chan"),
        ),
        check_vma=False,
    )
```

time: 1200 us -> 180 us (0.15)
  waiting for transfers between devices: 444 us -> 0 us
  blocking collectives: 353 us -> 0 us
  other arithmetic: 209 us -> 0.8 us
  Pallas kernels: 0 us -> 165 us
  between operations: 67.2 us -> 0.66 us
  matrix products: 56.4 us -> 0 us
  starting transfers between devices: 48.2 us -> 0 us
    psum x2 -> x0, blocking collectives: 332 us -> none  [the longest x1 326 us: body(): lax.psum((filter_part, gain_total, up_total, bias_total, down_total, scal...]
    psum x2 -> x0, waiting for transfers between devices: 206 us -> none  [the longest x1 167 us: body(): lax.psum((filter_part, gain_total, up_total, bias_total, down_total, scal...]
    pallas_call x0 -> x1, Pallas kernels: none -> 165 us  [block_call(): pl.pallas_call(functools.partial(kernel, side, shape4), out_shape=(jax.Sh...]
    reduce_sum x7 -> x0, other arithmetic: 122 us -> none  [the longest x1 61.2 us: body(): jnp.sum(filtered * filtered, -1)]
    all_gather x2 -> x0, waiting for transfers between devices: 108 us -> none  [the longest x1 63.5 us: body(): lax.all_gather(normed, 'chan', axis=2, tiled=True)]
    reduce_scatter x1 -> x0, waiting for transfers between devices: 82.9 us -> none  [body(): lax.psum_scatter(norm_part, 'chan', scatter_dimension=1, tiled=True)]
    dot_general x6 -> x0, matrix products: 56.4 us -> none  [the longest x1 14.1 us: mlp_backward(): jnp.dot(branch_grad, down_weight.T, preferred_element_type=jnp.float32)]
    ppermute x20 -> x0, starting transfers between devices: 48 us -> none  [shifted(): return lax.ppermute(block, axis, route)]
  transfers between devices with their start and end apart: 25 -> 0, of which waited for: 7 -> 0; matrix products, arithmetic and copies ran while one was open for 13% -> 0% of each run, Pallas kernels for 0% -> 0%
where the time goes in v1:
time: 180 us
  Pallas kernels  165 us (92%)
  local copies, waits for them, and re-layouts  13.9 us (8%)
    pallas_call x1, Pallas kernels, block_call(): pl.pallas_call(functools.partial(kernel, side, shape4), out_shape=(jax.Sh...  165 us
    unnamed x5, local copies, waits for them, and re-layouts  3.79 us

profile of v1, /device:TPU:1, one launch (start us, length us, event | category | flops | bytes accessed | tf_op | source)
XLA Modules:
  0.0 179.9 jit_solution(13342124694768398338)
XLA Ops:
  0.6 1.3 reshape.50.bias_ref
  1.9 0.8 convert_element_type.10
  2.7 0.1 convert_element_type.11
  2.8 1.4 copy.17.links
  4.2 2.7 %broadcast_in_dim.2.mask_ref = bf16[9216,128]{1,0:T(8,128)(2,1)} broadcast(bf16[9216]{0:T(1024)(128)(2,1)S(1)} %convert_element_type.11), dimensions={0} | broadcast | bytes 2377728 | tf_op jit(solution)/shard_map/broadcast_in_dim | solution.py:675
  6.9 164.6 %shard_map.153 = (bf16[9216,128]{1,0:T(8,128)(2,1)}, f32[2,256,512]{2,1,0:T(8,128)}, f32[64,128]{1,0:T(8,128)}) custom-call(s32[64,8]{1,0:T(8,128)} %copy.17.links, bf16[9216,128]{1,0:T(8,128)(2,1)} %bitcast.17, bf16[9216,128]{1,0:T(8,128)(2,1)} %bitcast.18, bf16[9216,128]{1,0:T(8,128)(2,1)} %broadcast_in_dim.2.mask_ref, f32[7,7,128]{2,1,0:T(8,128)} %depth_ref.1, ...), custom_call_target="tpu_custom_call" | custom-call | tf_op jit(solution)/shard_map/pallas_call | solution.py:635
  171.5 0.0 copy-start
  171.5 1.3 slice_bitcast_fusion.3
  172.8 1.2 slice_bitcast_fusion.2
  174.1 0.8 slice.18
  174.8 0.6 reshape.53
  175.4 2.1 %slice_bitcast_fusion = (f32[512,256]{0,1:T(8,128)S(1)}, f32[256,512]{1,0:T(8,128)}) fusion(f32[2,256,512]{2,1,0:T(8,128)} %get-tuple-element.12), kind=kLoop, calls=%fused_computation | loop fusion | bytes 2097152 | tf_op jit(solution)/shard_map/transpose | solution.py:686
  177.5 1.0 copy.18
  178.5 0.0 copy-done
  178.5 1.4 copy.20
Async XLA Ops:
  171.5 7.0 %copy-start = (bf16[9216,128]{1,0:T(8,128)(2,1)S(1)}, bf16[9216,128]{1,0:T(8,128)(2,1)}, u32[]{:S(2)}) copy-start(bf16[9216,128]{1,0:T(8,128)(2,1)} %get-tuple-element.10) | copy-start | bytes 7077892

commit v2 on v1

--- a/solution.py
+++ b/solution.py
@@ -51,11 +51,11 @@
 
 def kernel(
     side, shape4,
-    links, x_ref, c_ref, mask_ref, depth_ref, gamma_ref, up_ref, bias_ref, down_ref, scale_ref,
+    links, x_ref, c_ref, wet_ref, depth_ref, gamma_ref, up_ref, bias_ref, down_ref, scale_ref,
     out_ref, mats_ref, small_ref,
     pf, pg, taps, taps_acc, strips, corners, rows_in, cols_in, corners_in,
     wu, wd, pars, pars_in,
-    grad_own, grad_send, grad_in, y_own, y_send, y_in, conv_send, conv_in,
+    mask_ref, wet_turned, grad_own, grad_send, grad_in, y_all, y_in, conv_send, conv_in,
     sums, gamma_acc, bias_acc, ring_core, ring_a, ring_b, ring_y, total,
     small_a, small_peer, small_peer_in, small_core, small_x, small_z, small_y,
     halo_send, halo_recv, weight_sem, weight_recv, grad_sem, grad_recv, y_sem, y_recv, conv_sem, conv_recv,
@@ -122,26 +122,59 @@
     pars[0:1, :] = bias_ref[...].astype(F32)
     pars[1:2, 0:LANES] = gamma_ref[...].astype(F32)
     pars[2:3, 0:LANES] = scale_ref[...].astype(F32)
-    weight_copies = [
-        remote(pars, pars_in, weight_sem.at[0], weight_recv.at[0], peer),
-        remote(up_ref, wu.at[h], weight_sem.at[1], weight_recv.at[1], peer),
-        remote(down_ref, wd.at[h], weight_sem.at[2], weight_recv.at[2], peer),
-    ]
-    weight_arrivals = [
-        remote(pars, pars_in, weight_sem.at[0], weight_recv.at[0], peer),
-        remote(up_ref, wu.at[other], weight_sem.at[1], weight_recv.at[1], peer),
-        remote(down_ref, wd.at[other], weight_sem.at[2], weight_recv.at[2], peer),
-    ]
+    diagonal = y_dev(1, 1)
+    up_part, down_part = CHAN // 4, HALF_HIDDEN // 4
+
+    def part(ref, size, at, count=1):
+        return ref.at[pl.ds(pl.multiple_of(at * size, size), count * size), :]
+
+    def weight_copy(n, device, quarter, slot):
+        up = remote(
+            part(up_ref, up_part, quarter), part(wu.at[slot], up_part, quarter),
+            weight_sem.at[n], weight_recv.at[n], device,
+        )
+        down = remote(
+            part(down_ref, down_part, quarter), part(wd.at[slot], down_part, quarter),
+            weight_sem.at[n + 1], weight_recv.at[n + 1], device,
+        )
+        return [up, down]
+
+    pars_copy = remote(pars, pars_in, weight_sem.at[0], weight_recv.at[0], peer)
+    weight_copies = weight_copy(1, peer, 2 * core, h) + weight_copy(3, diagonal, 2 * core + 1, h)
+    weight_arrivals = weight_copy(1, peer, 2 * core, other) + weight_copy(3, diagonal, 2 * core + 1, other)
+
+    def weight_forward(half_at):
+        return [
+            remote(
+                part(wu.at[other], up_part, 2 * half_at, 2), part(wu.at[other], up_part, 2 * half_at, 2),
+                weight_sem.at[5], weight_recv.at[5], core_peer,
+            ),
+            remote(
+                part(wd.at[other], down_part, 2 * half_at, 2), part(wd.at[other], down_part, 2 * half_at, 2),
+                weight_sem.at[6], weight_recv.at[6], core_peer,
+            ),
+        ]
+
+    pars_copy.start()
     for copy in weight_copies:
         copy.start()
 
-    def fill_input(i, _):
-        at = pl.multiple_of(i * side, side)
-        to = pl.multiple_of((i + MARGIN) * width + 8, 8)
-        pf[pl.ds(to, side), :] = (x_ref[pl.ds(at, side), :] * mask_ref[pl.ds(at, side), :]).astype(F32)
-        return 0
-
-    lax.fori_loop(0, side, fill_input, 0)
+    wet_turned[...] = jnp.zeros_like(wet_turned)
+    wet_turned[0:side, 0:side] = wet_ref[...].astype(F32)
+    wet_turned[...] = wet_turned[...].T
+
+    def fill_input(g, _):
+        columns = pltpu.roll(wet_turned[0:side, :], (LANES - g * ROWS) % LANES, 1)
+        for t in range(ROWS):
+            i = g * ROWS + t
+            at = pl.ds(pl.multiple_of(i * side, side), side)
+            to = pl.multiple_of((i + MARGIN) * width + 8, 8)
+            wet = jnp.broadcast_to(columns[:, t : t + 1], (side, LANES))
+            mask_ref[at, :] = wet.astype(BF16)
+            pf[pl.ds(to, side), :] = x_ref[at, :].astype(F32) * wet
+        return 0
+
+    lax.fori_loop(0, side // ROWS, fill_input, 0)
 
     def make_strips(padded):
         for side_at, row in enumerate((MARGIN, side)):
@@ -175,7 +208,8 @@
         return copies
 
     def match(direction, source):
-        return jnp.logical_and(links[me, direction] == source, source >= 0).astype(F32)
+        link = links[pl.ds(me, 1), direction : direction + 1]
+        return jnp.where(jnp.logical_and(link == source, link >= 0), 1.0, 0.0)
 
     def fill_halo(padded, phase):
         for way, sign in enumerate((-1, 1)):
@@ -214,12 +248,18 @@
         at = pl.ds(pl.multiple_of(k * chunk, chunk), chunk)
         return remote(grad_send.at[at, :], grad_in.at[at, :], grad_sem.at[k], grad_recv.at[k], peer)
 
+    early = (steps + 1) // 2
+
     def fill_grad(k, _):
         there = pl.ds(pl.multiple_of(other * cells + k * chunk, chunk), chunk)
         here = pl.ds(pl.multiple_of(h * cells + k * chunk, chunk), chunk)
         at = pl.ds(pl.multiple_of(k * chunk, chunk), chunk)
         grad_send[at, :] = c_ref[there, :] * mask_ref[there, :]
-        grad_copy(k).start()
+
+        @pl.when(k < early)
+        def _():
+            grad_copy(k).start()
+
         grad_own[at, :] = c_ref[here, :] * mask_ref[here, :]
         return 0
 
@@ -230,9 +270,11 @@
             n = (a * KERNEL + b) * 8
             taps[n : n + 8, :] = jnp.broadcast_to(depth_ref[a, b : b + 1, :], (8, LANES))
 
-    for copy in forward_halo:
-        copy.wait_recv()
-    fill_halo(pf, 0)
+    for copy in weight_arrivals:
+        copy.wait_recv()
+    forwards = weight_forward(core)
+    for copy in forwards:
+        copy.start()
 
     def conv_block(padded, row, col, flip):
         base = row * width + col + 8 - MARGIN
@@ -255,42 +297,55 @@
 
     col_steps = side // (8 * COLS)
 
-    def conv_rows(start, put):
+    row_steps = side // ROWS
+    half_steps = row_steps // 2
+
+    def filter_forward(k, c):
+        col = pl.multiple_of(c * (8 * COLS), 8 * COLS)
+        acc = conv_block(pf, k * ROWS, col, False)
+        for i in range(ROWS):
+            at = pl.multiple_of((k * ROWS + i) * side + col, 8 * COLS)
+            y_all[pl.ds(at, 8 * COLS), :] = jnp.concatenate(acc[i], 0).astype(BF16)
+
+    def conv_inner(n, _):
+        filter_forward(1 + n // (col_steps - 2), 1 + n % (col_steps - 2))
+        return 0
+
+    lax.fori_loop(0, (row_steps - 2) * (col_steps - 2), conv_inner, 0)
+    for copy in forward_halo:
+        copy.wait_recv()
+    fill_halo(pf, 0)
+
+    def y_copy(k):
+        there = pl.ds(pl.multiple_of(other * cells + k * chunk, chunk), chunk)
+        at = pl.ds(pl.multiple_of(k * chunk, chunk), chunk)
+        return remote(y_all.at[there, :], y_in.at[at, :], y_sem.at[k], y_recv.at[k], peer)
+
+    def conv_outer(n, _):
+        away = n < half_steps
+        k = jnp.where(away, other * half_steps + n, h * half_steps + n - half_steps)
+        edge = jnp.logical_or(k == 0, k == row_steps - 1)
+
         def one(c, _):
-            col = pl.multiple_of(c * (8 * COLS), 8 * COLS)
-            acc = conv_block(pf, start, col, False)
-            for i in range(ROWS):
-                put(i, col, jnp.concatenate(acc[i], 0))
+            filter_forward(k, jnp.where(edge, c, c * (col_steps - 1)))
             return 0
 
-        lax.fori_loop(0, col_steps, one, 0)
-
-    def y_copy(k):
-        at = pl.ds(pl.multiple_of(k * chunk, chunk), chunk)
-        return remote(y_send.at[at, :], y_in.at[at, :], y_sem.at[k], y_recv.at[k], peer)
-
-    def conv_there(k, _):
-        def put(i, col, value):
-            at = pl.multiple_of((k * ROWS + i) * side + col, 8 * COLS)
-            y_send[pl.ds(at, 8 * COLS), :] = value.astype(BF16)
-
-        conv_rows(other * half + k * ROWS, put)
-        y_copy(k).start()
-        return 0
-
-    lax.fori_loop(0, steps, conv_there, 0)
-
-    def conv_here(k, _):
-        def put(i, col, value):
-            at = pl.multiple_of((k * ROWS + i) * side + col, 8 * COLS)
-            y_own[pl.ds(at, 8 * COLS), :] = value.astype(BF16)
-
-        conv_rows(h * half + k * ROWS, put)
-        return 0
-
-    lax.fori_loop(0, steps, conv_here, 0)
-
-    for copy in weight_arrivals:
+        lax.fori_loop(0, jnp.where(edge, col_steps, 2), one, 0)
+
+        @pl.when(away)
+        def _():
+            y_copy(n).start()
+
+        @pl.when(n + early < steps)
+        def _():
+            grad_copy(n + early).start()
+
+        return 0
+
+    lax.fori_loop(0, row_steps, conv_outer, 0)
+
+    pars_copy.wait_recv()
+    for copy in weight_forward(1 - core):
         copy.wait_recv()
     wu[h] = up_ref[...]
     wd[h] = down_ref[...]
@@ -319,7 +374,7 @@
         at = pl.ds(pl.multiple_of(k * chunk, chunk), chunk)
         y_copy(k).wait_recv()
         grad_copy(k).wait_recv()
-        low, high = ordered(y_own[at, :].astype(F32), y_in[at, :].astype(F32))
+        low, high = ordered(y_all[pl.ds(pl.multiple_of(h * cells + k * chunk, chunk), chunk), :].astype(F32), y_in[at, :].astype(F32))
         y = jnp.concatenate((low, high), 1)
         centred = y - jnp.sum(y, 1, keepdims=True) * (1.0 / CHAN)
         spread = jnp.sum(centred * centred, 1, keepdims=True) * (1.0 / CHAN)
@@ -389,36 +444,11 @@
     small_chan = remote(small_peer, small_peer_in, sm_send.at[0], sm_recv.at[0], peer)
     small_chan.start()
 
-    def take_conv(k, _):
-        conv_copy(k).wait_recv()
-        for i in range(MLP_ROWS):
-            at = pl.multiple_of((k * MLP_ROWS + i) * side, side)
-            to = pl.multiple_of((MARGIN + other * half + k * MLP_ROWS + i) * width + 8, 8)
-            pg[pl.ds(to, side), :] = conv_in[pl.ds(at, side), :].astype(F32)
-        return 0
-
-    lax.fori_loop(0, steps, take_conv, 0)
-    for copy in forward_halo:
-        copy.wait_send()
-    make_strips(pg)
-    backward_halo = halo_copies(1)
-    for copy in backward_halo:
-        copy.start()
-
-    rs_core.wait_recv()
-    sums[core] = sums[core] + ring_core[...]
-    a_rows, b_rows, y_rows = CHAN // n_x, CHAN // n_x // n_z, CHAN // n_x // n_z // 2
-    rs_a = []
-    for k, a in enumerate(a_peers):
-        piece = sums.at[core, pl.ds(pl.multiple_of(a * a_rows, a_rows), a_rows), :]
-        rs_a.append(remote(piece, ring_a.at[k], rs_send.at[1 + k], rs_recv.at[1 + k], dev(ring_tile(a, second))))
-    for copy in rs_a:
-        copy.start()
-
     taps_acc[...] = jnp.zeros_like(taps_acc)
 
     def filter_block(n, _):
-        row = (n // col_steps) * ROWS
+        line = n // col_steps
+        row = ((line + h * half_steps) % row_steps) * ROWS
         col = (n % col_steps) * (8 * COLS)
         inner = (row + MARGIN) * width + col + 8
         base = row * width + col + 8 - MARGIN
@@ -440,8 +470,37 @@
                 taps_acc[n : n + 8, :] += acc[a]
         return 0
 
-    blocks = (side // ROWS) * col_steps
-    lax.fori_loop(0, blocks // 2, filter_block, 0)
+    blocks = row_steps * col_steps
+    cuts = [blocks * n // 6 for n in range(7)]
+    lax.fori_loop(cuts[0], cuts[1], filter_block, 0)
+
+    rs_core.wait_recv()
+    sums[core] = sums[core] + ring_core[...]
+    a_rows, b_rows, y_rows = CHAN // n_x, CHAN // n_x // n_z, CHAN // n_x // n_z // 2
+    rs_a = []
+    for k, a in enumerate(a_peers):
+        piece = sums.at[core, pl.ds(pl.multiple_of(a * a_rows, a_rows), a_rows), :]
+        rs_a.append(remote(piece, ring_a.at[k], rs_send.at[1 + k], rs_recv.at[1 + k], dev(ring_tile(a, second))))
+    for copy in rs_a:
+        copy.start()
+
+    lax.fori_loop(cuts[1], cuts[2], filter_block, 0)
+
+    def take_conv(k, _):
+        conv_copy(k).wait_recv()
+        for i in range(MLP_ROWS):
+            at = pl.multiple_of((k * MLP_ROWS + i) * side, side)
+            to = pl.multiple_of((MARGIN + other * half + k * MLP_ROWS + i) * width + 8, 8)
+            pg[pl.ds(to, side), :] = conv_in[pl.ds(at, side), :].astype(F32)
+        return 0
+
+    lax.fori_loop(0, steps, take_conv, 0)
+    for copy in forward_halo:
+        copy.wait_send()
+    make_strips(pg)
+    backward_halo = halo_copies(1)
+    for copy in backward_halo:
+        copy.start()
 
     for copy in rs_a:
         copy.wait_recv()
@@ -454,7 +513,7 @@
     for copy in rs_b:
         copy.start()
 
-    lax.fori_loop(blocks // 2, blocks, filter_block, 0)
+    lax.fori_loop(cuts[2], cuts[3], filter_block, 0)
 
     for copy in rs_b:
         copy.wait_recv()
@@ -472,6 +531,29 @@
         rs_y.append(remote(piece, ring_y.at[k], rs_send.at[7 + k], rs_recv.at[7 + k], y_dev(dy, dc)))
     for copy in rs_y:
         copy.start()
+
+    lax.fori_loop(cuts[3], cuts[4], filter_block, 0)
+
+    for copy in rs_y:
+        copy.wait_recv()
+    y_start = b_start + at_yh * y_rows
+    y_at = pl.ds(pl.multiple_of(y_start, y_rows), y_rows)
+    total[core, y_at, :] = sums[y_piece(at_yh, h)] + (ring_y[0] + ring_y[1] + ring_y[2])
+    y_mate = dev(tile_at((at_yh + 1) % 2, at_z, at_x, core))
+    ag_y = remote(total.at[core, y_at, :], total.at[core, y_at, :], ag_send.at[0], ag_recv.at[0], y_mate)
+    ag_y.start()
+
+    lax.fori_loop(cuts[4], cuts[5], filter_block, 0)
+
+    ag_y.wait_recv()
+    ag_b = []
+    for k, b in enumerate(b_peers):
+        block = total.at[core, b_at, :]
+        ag_b.append(remote(block, block, ag_send.at[1 + k], ag_recv.at[1 + k], dev(ring_tile(first, b))))
+    for copy in ag_b:
+        copy.start()
+
+    lax.fori_loop(cuts[5], cuts[6], filter_block, 0)
 
     for n in range(n_taps):
         small_a[n : n + 1, :] = jnp.sum(taps_acc[n * 8 : n * 8 + 8, :], 0, keepdims=True)
@@ -501,18 +583,18 @@
         lax.fori_loop(0, col_steps, one, 0)
         return 0
 
-    row_steps = side // ROWS
     marks = [row_steps * n // 4 for n in range(5)]
     lax.fori_loop(marks[0], marks[1], input_rows, 0)
 
-    for copy in rs_y:
-        copy.wait_recv()
-    y_start = b_start + at_yh * y_rows
-    y_at = pl.ds(pl.multiple_of(y_start, y_rows), y_rows)
-    total[core, y_at, :] = sums[y_piece(at_yh, h)] + (ring_y[0] + ring_y[1] + ring_y[2])
-    y_mate = dev(tile_at((at_yh + 1) % 2, at_z, at_x, core))
-    ag_y = remote(total.at[core, y_at, :], total.at[core, y_at, :], ag_send.at[0], ag_recv.at[0], y_mate)
-    ag_y.start()
+    for copy in ag_b:
+        copy.wait_recv()
+    ag_a = []
+    for k, a in enumerate(a_peers):
+        block = total.at[core, a_at, :]
+        ag_a.append(remote(block, block, ag_send.at[4 + k], ag_recv.at[4 + k], dev(ring_tile(a, second))))
+    for copy in ag_a:
+        copy.start()
+
     sm_core.wait_recv()
 
     def small_stage(ref, value, at, size, base, tile):
@@ -532,13 +614,11 @@
     )
     lax.fori_loop(marks[1], marks[2], input_rows, 0)
 
-    ag_y.wait_recv()
-    ag_b = []
-    for k, b in enumerate(b_peers):
-        block = total.at[core, b_at, :]
-        ag_b.append(remote(block, block, ag_send.at[1 + k], ag_recv.at[1 + k], dev(ring_tile(first, b))))
-    for copy in ag_b:
-        copy.start()
+    for copy in ag_a:
+        copy.wait_recv()
+    ag_core = remote(total.at[core], total.at[core], ag_send.at[7], ag_recv.at[7], core_peer)
+    ag_core.start()
+
     for copy in sm_x:
         copy.wait_recv()
     sm_z = small_stage(
@@ -546,33 +626,20 @@
     )
     lax.fori_loop(marks[2], marks[3], input_rows, 0)
 
-    for copy in ag_b:
-        copy.wait_recv()
-    ag_a = []
-    for k, a in enumerate(a_peers):
-        block = total.at[core, a_at, :]
-        ag_a.append(remote(block, block, ag_send.at[4 + k], ag_recv.at[4 + k], dev(ring_tile(a, second))))
-    for copy in ag_a:
-        copy.start()
     for copy in sm_z:
         copy.wait_recv()
     sm_y = small_stage(
         small_y, sum(small_z[k] for k in range(n_z)), at_yh, 2, 8, lambda yh: tile_at(yh, at_z, at_x, core)
     )
-    lax.fori_loop(marks[3], marks[4], input_rows, 0)
-
-    for copy in ag_a:
-        copy.wait_recv()
-    ag_core = remote(total.at[core], total.at[core], ag_send.at[7], ag_recv.at[7], core_peer)
-    ag_core.start()
-    for copy in sm_y:
-        copy.wait_recv()
-    small_ref[...] = (small_y[0] + small_y[1]) * q
     mats_ref[core] = total[core] * q
     ag_core.wait_recv()
     mats_ref[1 - core] = total[1 - core] * q
-
-    for copy in weight_copies + backward_halo + [rs_core, small_chan, sm_core, ag_y, ag_core]:
+    lax.fori_loop(marks[3], marks[4], input_rows, 0)
+    for copy in sm_y:
+        copy.wait_recv()
+    small_ref[...] = (small_y[0] + small_y[1]) * q
+
+    for copy in weight_copies + forwards + backward_halo + [pars_copy, rs_core, small_chan, sm_core, ag_y, ag_core]:
         copy.wait_send()
     for copy in rs_a + rs_b + rs_y + ag_a + ag_b + sm_x + sm_z + sm_y:
         copy.wait_send()
@@ -589,7 +656,7 @@
 SHAPES = {64: (2, 4, 4, 2), 16: (2, 2, 2, 2)}
 
 
-def block_call(inputs, cotangent, mask, neighbours, depth_weight, gamma, up_weight, up_bias, down_weight, layer_scale):
+def block_call(inputs, cotangent, wet, neighbours, depth_weight, gamma, up_weight, up_bias, down_weight, layer_scale):
     side = inputs.shape[1]
     half_chan = inputs.shape[3]
     flat = (side * side, half_chan)
@@ -599,7 +666,7 @@
     cells = side * side // 2
     steps = side // 2 // MLP_ROWS
     a_rows = CHAN // n_x
-    vmem, smem = pltpu.VMEM, pl.BlockSpec(memory_space=pltpu.SMEM)
+    vmem = pltpu.VMEM
     whole = pl.BlockSpec(memory_space=pltpu.VMEM)
     dma = pltpu.SemaphoreType.DMA
     padded = vmem(((side + 2 * MARGIN) * width, LANES), F32)
@@ -617,7 +684,8 @@
         vmem((2, CHAN, HALF_HIDDEN), BF16),
         vmem((2, HALF_HIDDEN, CHAN), BF16),
         pars, pars,
-        piece, piece, piece, piece, piece, piece, piece, piece,
+        vmem((side * side, LANES), BF16), vmem((LANES, LANES), F32),
+        piece, piece, piece, vmem((side * side, LANES), BF16), piece, piece, piece,
         vmem((2, CHAN, HIDDEN), F32),
         vmem((8, CHAN), F32),
         vmem((8, HIDDEN), F32),
@@ -628,7 +696,7 @@
         vmem((2, CHAN, HALF_HIDDEN), F32),
         small, vmem((8, LANES), F32), vmem((8, LANES), F32), small,
         vmem((n_x, 64, LANES), F32), vmem((n_z, 64, LANES), F32), vmem((2, 64, LANES), F32),
-        dma((2, 12)), dma((2, 12)), dma((3,)), dma((3,)),
+        dma((2, 12)), dma((2, 12)), dma((7,)), dma((7,)),
         dma((steps,)), dma((steps,)), dma((steps,)), dma((steps,)), dma((steps,)), dma((steps,)),
         dma((10,)), dma((10,)), dma((8,)), dma((8,)), dma((9,)), dma((9,)),
     ]
@@ -639,7 +707,7 @@
             jax.ShapeDtypeStruct((2, CHAN, HALF_HIDDEN), F32),
             jax.ShapeDtypeStruct((64, LANES), F32),
         ),
-        in_specs=[smem] + [whole] * 9,
+        in_specs=[whole] * 10,
         out_specs=(whole, whole, whole),
         scratch_shapes=scratch,
         compiler_params=pltpu.CompilerParams(
@@ -649,7 +717,7 @@
         neighbours,
         inputs.reshape(flat),
         cotangent.reshape(flat),
-        mask,
+        wet[0],
         depth_weight,
         gamma.reshape(1, half_chan),
         up_weight,
@@ -671,10 +739,8 @@
     down_weight,
     layer_scale,
 ):
-    side = inputs.shape[1]
-    mask = jnp.broadcast_to(wet[0].astype(BF16)[..., None], (side, side, LANES)).reshape(side * side, LANES)
     grad, mats, small = block_call(
-        inputs, cotangent, mask, neighbours, depth_weight, gamma, up_weight, up_bias, down_weight, layer_scale
+        inputs, cotangent, wet, neighbours, depth_weight, gamma, up_weight, up_bias, down_weight, layer_scale
     )
     taps = KERNEL * KERNEL
     return (

time: 180 us -> 154 us (0.86)
  Pallas kernels: 165 us -> 141 us
  local copies, waits for them, and re-layouts: 13.9 us -> 11.1 us
    pallas_call x1, Pallas kernels: 165 us -> 141 us  [block_call(): pl.pallas_call(functools.partial(kernel, side, shape4), out_shape=(jax.Sh...]
    broadcast_in_dim x1 -> x0, local copies, waits for them, and re-layouts: 2.7 us -> none  [body(): jnp.broadcast_to(wet[0].astype(BF16)[..., None], (side, side, LANES))]
where the time goes in v2:
time: 154 us; the launch traced here: 152 us
  Pallas kernels  141 us (92%)
  local copies, waits for them, and re-layouts  11.1 us (7%)
    pallas_call x1, Pallas kernels, block_call(): pl.pallas_call(functools.partial(kernel, side, shape4), out_shape=(jax.Sh...  141 us
    unnamed x5, local copies, waits for them, and re-layouts  3.79 us

profile of v2, /device:TPU:1, one launch (start us, length us, event | category | flops | bytes accessed | tf_op | source)
XLA Modules:
  0.0 152.3 jit_solution(17067132432856471075)
XLA Ops:
  0.6 1.4 copy.17.links
  2.0 1.3 reshape.41.bias_ref
  3.3 140.6 %shard_map.153 = (bf16[9216,128]{1,0:T(8,128)(2,1)}, f32[2,256,512]{2,1,0:T(8,128)}, f32[64,128]{1,0:T(8,128)}) custom-call(s32[64,8]{1,0:T(8,128)} %copy.17.links, bf16[9216,128]{1,0:T(8,128)(2,1)} %bitcast.18, bf16[9216,128]{1,0:T(8,128)(2,1)} %bitcast.19, s32[96,96]{1,0:T(8,128)} %bitcast.21, f32[7,7,128]{2,1,0:T(8,128)} %depth_ref.1, ...), custom_call_target="tpu_custom_call" | custom-call | tf_op jit(solution)/shard_map/pallas_call | solution.py:703
  143.9 0.0 copy-start
  143.9 1.3 slice_bitcast_fusion.3
  145.2 0.8 slice.18
  146.0 0.6 reshape.44
  146.6 1.2 slice_bitcast_fusion.2
  147.8 2.1 %slice_bitcast_fusion = (f32[512,256]{0,1:T(8,128)S(1)}, f32[256,512]{1,0:T(8,128)}) fusion(f32[2,256,512]{2,1,0:T(8,128)} %get-tuple-element.12), kind=kLoop, calls=%fused_computation | loop fusion | bytes 2097152 | tf_op jit(solution)/shard_map/transpose | solution.py:752
  149.9 1.0 copy.18
  150.9 0.0 copy-done
  150.9 1.4 copy.20
Async XLA Ops:
  143.9 7.0 %copy-start = (bf16[9216,128]{1,0:T(8,128)(2,1)S(1)}, bf16[9216,128]{1,0:T(8,128)(2,1)}, u32[]{:S(2)}) copy-start(bf16[9216,128]{1,0:T(8,128)(2,1)} %get-tuple-element.10) | copy-start | bytes 7077892

commit v3 on v2

--- a/solution.py
+++ b/solution.py
@@ -17,12 +17,12 @@
 BLOCK = 256
 ROWS = 8
 COLS = 2
-MLP_ROWS = 8
 REACH = 5
 F32 = jnp.float32
 BF16 = jnp.bfloat16
 MESH = pl.DeviceIdType.MESH
 density = 0.3989422804014327
+half_log2 = -0.7213475204444817
 
 
 def gelu_pieces(hidden):
@@ -30,7 +30,7 @@
     denom = 1.0 + 0.2316419 * size
     inverse = pl.reciprocal(denom, approx=True)
     inverse = inverse * (2.0 - denom * inverse)
-    bell = jnp.exp(-0.5 * hidden * hidden)
+    bell = jnp.exp2(hidden * hidden * half_log2)
     poly = 0.5 * 1.061405429
     for factor in (-1.453152027, 1.421413741, -0.284496736, 0.254829592):
         poly = poly * inverse + 0.5 * factor
@@ -51,11 +51,12 @@
 
 def kernel(
     side, shape4,
-    links, x_ref, c_ref, wet_ref, depth_ref, gamma_ref, up_ref, bias_ref, down_ref, scale_ref,
-    out_ref, mats_ref, small_ref,
+    links_in, x_in, c_in, wet_ref, depth_ref, gamma_ref, up_ref, bias_ref, down_ref, scale_ref,
+    out_ref, taps_ref, gain_ref, up_sum_ref, bias_sum_ref, down_sum_ref, scale_sum_ref,
+    links, x_ref, c_ref, out_tile, load_sem, out_sem,
     pf, pg, taps, taps_acc, strips, corners, rows_in, cols_in, corners_in,
     wu, wd, pars, pars_in,
-    mask_ref, wet_turned, grad_own, grad_send, grad_in, y_all, y_in, conv_send, conv_in,
+    mask_ref, wet_turned, grad_in, y_all, y_in, conv_send, conv_in,
     sums, gamma_acc, bias_acc, ring_core, ring_a, ring_b, ring_y, total,
     small_a, small_peer, small_peer_in, small_core, small_x, small_z, small_y,
     halo_send, halo_recv, weight_sem, weight_recv, grad_sem, grad_recv, y_sem, y_recv, conv_sem, conv_recv,
@@ -63,11 +64,10 @@
 ):
     n_yh, n_z, n_x, n_core = shape4
     tiles = n_yh * n_z * n_x * n_core
-    half = side // 2
     width = side + 16
-    cells = half * side
-    steps = half // MLP_ROWS
-    chunk = MLP_ROWS * side
+    row_steps = side // ROWS
+    steps = row_steps // 2
+    chunk = ROWS * side
     me = lax.axis_index("tiles")
     h = lax.axis_index("chan")
     other = 1 - h
@@ -88,6 +88,12 @@
             src_ref=src, dst_ref=dst, send_sem=send, recv_sem=recv, device_id=device, device_id_type=MESH
         )
 
+    def line_at(which, k):
+        return k + which * (row_steps - 1 - 2 * k)
+
+    def chunk_rows(line):
+        return pl.ds(pl.multiple_of(line * chunk, chunk), chunk)
+
     first = core * at_z + (1 - core) * at_x
     second = core * at_x + (1 - core) * at_z
 
@@ -116,12 +122,24 @@
     targets += [y_dev(dy, dc) for dy, dc in y_peers]
     for target in targets:
         pl.semaphore_signal(barrier, inc=1, device_id=target, device_id_type=MESH)
+    loads = [
+        pltpu.make_async_copy(x_in, x_ref, load_sem.at[0]),
+        pltpu.make_async_copy(c_in, c_ref, load_sem.at[1]),
+        pltpu.make_async_copy(up_ref, wu.at[h], load_sem.at[2]),
+        pltpu.make_async_copy(down_ref, wd.at[h], load_sem.at[3]),
+        pltpu.make_async_copy(links_in, links, load_sem.at[4]),
+    ]
+    for copy in loads:
+        copy.start()
+    pars[...] = jnp.zeros_like(pars)
+    pars[0:1, :] = bias_ref[...].astype(F32).reshape(1, HALF_HIDDEN)
+    pars[1:2, 0:LANES] = gamma_ref[...].astype(F32).reshape(1, LANES)
+    pars[2:3, 0:LANES] = scale_ref[...].astype(F32).reshape(1, LANES)
+    wet_turned[...] = jnp.zeros_like(wet_turned)
+    wet_turned[0:side, 0:side] = wet_ref[...].astype(F32)
+    wet_turned[...] = wet_turned[...].T
     pl.semaphore_wait(barrier, len(targets))
 
-    pars[...] = jnp.zeros_like(pars)
-    pars[0:1, :] = bias_ref[...].astype(F32)
-    pars[1:2, 0:LANES] = gamma_ref[...].astype(F32)
-    pars[2:3, 0:LANES] = scale_ref[...].astype(F32)
     diagonal = y_dev(1, 1)
     up_part, down_part = CHAN // 4, HALF_HIDDEN // 4
 
@@ -159,10 +177,18 @@
     for copy in weight_copies:
         copy.start()
 
-    wet_turned[...] = jnp.zeros_like(wet_turned)
-    wet_turned[0:side, 0:side] = wet_ref[...].astype(F32)
-    wet_turned[...] = wet_turned[...].T
-
+    early = min(4, steps)
+
+    def grad_copy(k):
+        return remote(
+            c_in.at[chunk_rows(line_at(other, k)), :], grad_in.at[chunk_rows(k), :],
+            grad_sem.at[k], grad_recv.at[k], peer,
+        )
+
+    for k in range(early):
+        grad_copy(k).start()
+
+    loads[0].wait()
     def fill_input(g, _):
         columns = pltpu.roll(wet_turned[0:side, :], (LANES - g * ROWS) % LANES, 1)
         for t in range(ROWS):
@@ -176,19 +202,21 @@
 
     lax.fori_loop(0, side // ROWS, fill_input, 0)
 
-    def make_strips(padded):
+    def row_strips(padded):
         for side_at, row in enumerate((MARGIN, side)):
             for k in range(MARGIN):
                 base = (row + k) * width + 8
                 strips[side_at, k * side : (k + 1) * side, :] = padded[base : base + side, :].astype(BF16)
                 near = base if side_at == 0 else base + side - 16
                 corners[side_at, k * 16 : (k + 1) * 16, :] = padded[near : near + 16, :].astype(BF16)
+
+    def col_strips(padded):
         for side_at, col in enumerate((8, 8 + side - MARGIN)):
             for k in range(MARGIN):
                 line = padded[pl.ds(MARGIN * width + col + k, side, stride=width), :]
                 strips[2 + side_at, k * side : (k + 1) * side, :] = line.astype(BF16)
 
-    def halo_copies(phase):
+    def row_copies(phase):
         copies = []
         for n, (sign, d) in enumerate(halo):
             device = dev(halo_tile(sign, d))
@@ -199,6 +227,10 @@
                 copies.append(remote(strips.at[1 - way], rows_in.at[phase, way, d - 1], send, recv, device))
             else:
                 copies.append(remote(corners.at[1 - way], corners_in.at[phase, way], send, recv, device))
+        return copies
+
+    def col_copies(phase):
+        copies = []
         for way, sign in enumerate((1, -1)):
             device = dev(halo_tile(sign, 1))
             n = len(halo) + way
@@ -239,31 +271,12 @@
                 line = cols_in[phase, way, k * side : (k + 1) * side, :].astype(F32)
                 padded[pl.ds(MARGIN * width + col + k, side, stride=width), :] = line * hit
 
-    make_strips(pf)
-    forward_halo = halo_copies(0)
+    row_strips(pf)
+    col_strips(pf)
+    forward_halo = row_copies(0) + col_copies(0)
     for copy in forward_halo:
         copy.start()
-
-    def grad_copy(k):
-        at = pl.ds(pl.multiple_of(k * chunk, chunk), chunk)
-        return remote(grad_send.at[at, :], grad_in.at[at, :], grad_sem.at[k], grad_recv.at[k], peer)
-
-    early = (steps + 1) // 2
-
-    def fill_grad(k, _):
-        there = pl.ds(pl.multiple_of(other * cells + k * chunk, chunk), chunk)
-        here = pl.ds(pl.multiple_of(h * cells + k * chunk, chunk), chunk)
-        at = pl.ds(pl.multiple_of(k * chunk, chunk), chunk)
-        grad_send[at, :] = c_ref[there, :] * mask_ref[there, :]
-
-        @pl.when(k < early)
-        def _():
-            grad_copy(k).start()
-
-        grad_own[at, :] = c_ref[here, :] * mask_ref[here, :]
-        return 0
-
-    lax.fori_loop(0, steps, fill_grad, 0)
+    loads[4].wait()
 
     for a in range(KERNEL):
         for b in range(KERNEL):
@@ -297,9 +310,6 @@
 
     col_steps = side // (8 * COLS)
 
-    row_steps = side // ROWS
-    half_steps = row_steps // 2
-
     def filter_forward(k, c):
         col = pl.multiple_of(c * (8 * COLS), 8 * COLS)
         acc = conv_block(pf, k * ROWS, col, False)
@@ -317,13 +327,13 @@
     fill_halo(pf, 0)
 
     def y_copy(k):
-        there = pl.ds(pl.multiple_of(other * cells + k * chunk, chunk), chunk)
-        at = pl.ds(pl.multiple_of(k * chunk, chunk), chunk)
-        return remote(y_all.at[there, :], y_in.at[at, :], y_sem.at[k], y_recv.at[k], peer)
+        return remote(
+            y_all.at[chunk_rows(line_at(other, k)), :], y_in.at[chunk_rows(k), :], y_sem.at[k], y_recv.at[k], peer
+        )
 
     def conv_outer(n, _):
-        away = n < half_steps
-        k = jnp.where(away, other * half_steps + n, h * half_steps + n - half_steps)
+        away = n < steps
+        k = jnp.where(away, line_at(other, n), line_at(h, n - steps))
         edge = jnp.logical_or(k == 0, k == row_steps - 1)
 
         def one(c, _):
@@ -347,8 +357,10 @@
     pars_copy.wait_recv()
     for copy in weight_forward(1 - core):
         copy.wait_recv()
-    wu[h] = up_ref[...]
-    wd[h] = down_ref[...]
+    for copy in loads[1:4]:
+        copy.wait()
+    for copy in forward_halo:
+        copy.wait_send()
     mine = h == 0
 
     def ordered(own, others):
@@ -365,26 +377,64 @@
     sums[...] = jnp.zeros_like(sums)
     gamma_acc[...] = jnp.zeros_like(gamma_acc)
     bias_acc[...] = jnp.zeros_like(bias_acc)
+    taps_acc[...] = jnp.zeros_like(taps_acc)
 
     def conv_copy(k):
-        at = pl.ds(pl.multiple_of(k * chunk, chunk), chunk)
+        at = chunk_rows(k)
         return remote(conv_send.at[at, :], conv_in.at[at, :], conv_sem.at[k], conv_recv.at[k], peer)
 
+    def take_conv(k):
+        conv_copy(k).wait_recv()
+        for i in range(ROWS):
+            at = pl.multiple_of((k * ROWS + i) * side, side)
+            to = pl.multiple_of((MARGIN + line_at(other, k) * ROWS + i) * width + 8, 8)
+            pg[pl.ds(to, side), :] = conv_in[pl.ds(at, side), :].astype(F32)
+
+    def filter_line(line):
+        row = line * ROWS
+
+        def one(c, _):
+            col = c * (8 * COLS)
+            inner = (row + MARGIN) * width + col + 8
+            base = row * width + col + 8 - MARGIN
+            grads = [
+                [pg[pl.ds(pl.multiple_of(inner, 8) + (i * width + v * 8), 8), :] for v in range(COLS)] for i in range(ROWS)
+            ]
+            for b in range(KERNEL):
+                acc = [None] * KERNEL
+                for r in range(ROWS + KERNEL - 1):
+                    for v in range(COLS):
+                        value = pf[pl.ds(base + (r * width + v * 8 + b), 8), :]
+                        for a in range(KERNEL):
+                            i = r - a
+                            if 0 <= i < ROWS:
+                                term = value * grads[i][v]
+                                acc[a] = term if acc[a] is None else acc[a] + term
+                for a in range(KERNEL):
+                    n = (a * KERNEL + b) * 8
+                    taps_acc[n : n + 8, :] += acc[a]
+            return 0
+
+        lax.fori_loop(0, col_steps, one, 0)
+
     def mlp(k, _):
-        at = pl.ds(pl.multiple_of(k * chunk, chunk), chunk)
+        at = chunk_rows(k)
+        line = line_at(h, k)
+        own_at = chunk_rows(line)
         y_copy(k).wait_recv()
         grad_copy(k).wait_recv()
-        low, high = ordered(y_all[pl.ds(pl.multiple_of(h * cells + k * chunk, chunk), chunk), :].astype(F32), y_in[at, :].astype(F32))
+        low, high = ordered(y_all[own_at, :].astype(F32), y_in[at, :].astype(F32))
         y = jnp.concatenate((low, high), 1)
         centred = y - jnp.sum(y, 1, keepdims=True) * (1.0 / CHAN)
         spread = jnp.sum(centred * centred, 1, keepdims=True) * (1.0 / CHAN)
         inv_spread = lax.rsqrt(spread + 1e-06)
         unit = centred * inv_spread
         normed = (unit * gamma_row).astype(BF16)
-        low, high = ordered(grad_own[at, :].astype(F32), grad_in[at, :].astype(F32))
-        branch_grad = (jnp.concatenate((low, high), 1) * scale_row).astype(BF16)
+        wet = mask_ref[own_at, :].astype(F32)
+        low, high = ordered(c_ref[own_at, :].astype(F32), grad_in[at, :].astype(F32))
+        branch_grad = (jnp.concatenate((low * wet, high * wet), 1) * scale_row).astype(BF16)
         branch_t = branch_grad.T
-        normed_t = normed.T
+        normed_t = jnp.concatenate((normed.T, jnp.ones((16, chunk), BF16)), 0)
         norm_grad = jnp.zeros((chunk, CHAN), F32)
         for block in range(HIDDEN // BLOCK):
             slot, off = divmod(block * BLOCK, HALF_HIDDEN)
@@ -395,8 +445,9 @@
             activated, slope = gelu_pieces(hidden)
             hidden_grad = (nt(branch_grad, w_down) * slope).astype(BF16)
             sums[1, :, cols] += nn(branch_t, activated.astype(BF16))
-            sums[0, :, cols] += nn(normed_t, hidden_grad)
-            bias_acc[:, cols] += jnp.sum(hidden_grad.astype(F32).reshape(chunk // 8, 8, BLOCK), 0)
+            up_terms = nn(normed_t, hidden_grad)
+            sums[0, :, cols] += up_terms[:CHAN]
+            bias_acc[:, cols] += up_terms[CHAN : CHAN + 8]
             norm_grad = norm_grad + nt(hidden_grad, w_up)
         gamma_acc[...] += jnp.sum((norm_grad * unit).reshape(chunk // 8, 8, CHAN), 0)
         scaled = norm_grad * gamma_row
@@ -406,9 +457,18 @@
         own, away = ordered(conv_grad[:, :LANES], conv_grad[:, LANES:])
         conv_send[at, :] = away.astype(BF16)
         conv_copy(k).start()
-        for i in range(MLP_ROWS):
-            to = pl.multiple_of((MARGIN + h * half + k * MLP_ROWS + i) * width + 8, 8)
+        for i in range(ROWS):
+            to = pl.multiple_of((MARGIN + line * ROWS + i) * width + 8, 8)
             pg[pl.ds(to, side), :] = own[i * side : (i + 1) * side]
+        filter_line(line)
+
+        @pl.when(k == steps // 2)
+        def _():
+            take_conv(0)
+            row_strips(pg)
+            for copy in row_copies(1):
+                copy.start()
+
         return 0
 
     lax.fori_loop(0, steps, mlp, 0)
@@ -426,7 +486,7 @@
         paired = paired + nn(down_high[:, cols], wd[slot]) + nn(down_low[:, cols], wd[slot])
     scale_sum = jnp.sum(jnp.where(ident, paired, 0.0), 0, keepdims=True) / scale_row
     gamma_sum = jnp.sum(gamma_acc[...], 0, keepdims=True)
-    bias_sum = jnp.sum(bias_acc[...], 0, keepdims=True)
+    bias_sum = bias_acc[0:1, :]
     small_peer[...] = jnp.zeros_like(small_peer)
     small_a[...] = jnp.zeros_like(small_a)
     n_taps = KERNEL * KERNEL
@@ -444,35 +504,50 @@
     small_chan = remote(small_peer, small_peer_in, sm_send.at[0], sm_recv.at[0], peer)
     small_chan.start()
 
-    taps_acc[...] = jnp.zeros_like(taps_acc)
-
-    def filter_block(n, _):
-        line = n // col_steps
-        row = ((line + h * half_steps) % row_steps) * ROWS
-        col = (n % col_steps) * (8 * COLS)
-        inner = (row + MARGIN) * width + col + 8
-        base = row * width + col + 8 - MARGIN
-        grads = [
-            [pg[pl.ds(pl.multiple_of(inner, 8) + (i * width + v * 8), 8), :] for v in range(COLS)] for i in range(ROWS)
-        ]
-        for b in range(KERNEL):
-            acc = [None] * KERNEL
-            for r in range(ROWS + KERNEL - 1):
-                for v in range(COLS):
-                    value = pf[pl.ds(base + (r * width + v * 8 + b), 8), :]
-                    for a in range(KERNEL):
-                        i = r - a
-                        if 0 <= i < ROWS:
-                            term = value * grads[i][v]
-                            acc[a] = term if acc[a] is None else acc[a] + term
-            for a in range(KERNEL):
-                n = (a * KERNEL + b) * 8
-                taps_acc[n : n + 8, :] += acc[a]
+    def input_block(line, c):
+        row = line * ROWS
+        col = pl.multiple_of(c * (8 * COLS), 8 * COLS)
+        acc = conv_block(pg, row, col, True)
+        for i in range(ROWS):
+            at = pl.ds(pl.multiple_of((row + i) * side + col, 8 * COLS), 8 * COLS)
+            wet = mask_ref[at, :].astype(F32)
+            grad = c_ref[at, :].astype(F32)
+            out_tile[at, :] = (wet * (grad + jnp.concatenate(acc[i], 0))).astype(BF16)
+
+    inner_cols = col_steps - 2
+
+    def own_inner(n, _):
+        input_block(line_at(h, 1 + n // inner_cols), 1 + n % inner_cols)
         return 0
 
-    blocks = row_steps * col_steps
-    cuts = [blocks * n // 6 for n in range(7)]
-    lax.fori_loop(cuts[0], cuts[1], filter_block, 0)
+    def rest_inner(n, _):
+        k = n // inner_cols
+        input_block(jnp.where(k == 0, line_at(h, steps - 1), line_at(other, k)), 1 + n % inner_cols)
+        return 0
+
+    def out_copy(k):
+        return pltpu.make_async_copy(out_tile.at[chunk_rows(k), :], out_ref.at[chunk_rows(k), :], out_sem.at[k])
+
+    def input_edges(k, _):
+        edge = jnp.logical_or(k == 0, k == row_steps - 1)
+
+        def one(c, _):
+            input_block(k, jnp.where(edge, c, c * (col_steps - 1)))
+            return 0
+
+        lax.fori_loop(0, jnp.where(edge, col_steps, 2), one, 0)
+        out_copy(k).start()
+        return 0
+
+    def peer_line(k, _):
+        @pl.when(k > 0)
+        def _():
+            take_conv(k)
+
+        filter_line(line_at(other, k))
+        return 0
+
+    lax.fori_loop(0, (steps - 2) * inner_cols, own_inner, 0)
 
     rs_core.wait_recv()
     sums[core] = sums[core] + ring_core[...]
@@ -484,23 +559,8 @@
     for copy in rs_a:
         copy.start()
 
-    lax.fori_loop(cuts[1], cuts[2], filter_block, 0)
-
-    def take_conv(k, _):
-        conv_copy(k).wait_recv()
-        for i in range(MLP_ROWS):
-            at = pl.multiple_of((k * MLP_ROWS + i) * side, side)
-            to = pl.multiple_of((MARGIN + other * half + k * MLP_ROWS + i) * width + 8, 8)
-            pg[pl.ds(to, side), :] = conv_in[pl.ds(at, side), :].astype(F32)
-        return 0
-
-    lax.fori_loop(0, steps, take_conv, 0)
-    for copy in forward_halo:
-        copy.wait_send()
-    make_strips(pg)
-    backward_halo = halo_copies(1)
-    for copy in backward_halo:
-        copy.start()
+    lax.fori_loop(0, 2, peer_line, 0)
+    lax.fori_loop(2, steps - 2, peer_line, 0)
 
     for copy in rs_a:
         copy.wait_recv()
@@ -513,7 +573,7 @@
     for copy in rs_b:
         copy.start()
 
-    lax.fori_loop(cuts[2], cuts[3], filter_block, 0)
+    lax.fori_loop(steps - 2, steps - 1, peer_line, 0)
 
     for copy in rs_b:
         copy.wait_recv()
@@ -532,28 +592,12 @@
     for copy in rs_y:
         copy.start()
 
-    lax.fori_loop(cuts[3], cuts[4], filter_block, 0)
-
-    for copy in rs_y:
-        copy.wait_recv()
-    y_start = b_start + at_yh * y_rows
-    y_at = pl.ds(pl.multiple_of(y_start, y_rows), y_rows)
-    total[core, y_at, :] = sums[y_piece(at_yh, h)] + (ring_y[0] + ring_y[1] + ring_y[2])
-    y_mate = dev(tile_at((at_yh + 1) % 2, at_z, at_x, core))
-    ag_y = remote(total.at[core, y_at, :], total.at[core, y_at, :], ag_send.at[0], ag_recv.at[0], y_mate)
-    ag_y.start()
-
-    lax.fori_loop(cuts[4], cuts[5], filter_block, 0)
-
-    ag_y.wait_recv()
-    ag_b = []
-    for k, b in enumerate(b_peers):
-        block = total.at[core, b_at, :]
-        ag_b.append(remote(block, block, ag_send.at[1 + k], ag_recv.at[1 + k], dev(ring_tile(first, b))))
-    for copy in ag_b:
-        copy.start()
-
-    lax.fori_loop(cuts[5], cuts[6], filter_block, 0)
+    take_conv(steps - 1)
+    col_strips(pg)
+    last_halo = col_copies(1)
+    for copy in last_halo:
+        copy.start()
+    filter_line(line_at(other, steps - 1))
 
     for n in range(n_taps):
         small_a[n : n + 1, :] = jnp.sum(taps_acc[n * 8 : n * 8 + 8, :], 0, keepdims=True)
@@ -563,36 +607,24 @@
     sm_core = remote(small_a, small_core, sm_send.at[1], sm_recv.at[1], core_peer)
     sm_core.start()
 
-    for copy in backward_halo:
-        copy.wait_recv()
-    fill_halo(pg, 1)
-
-    def input_rows(k, _):
-        row = k * ROWS
-
-        def one(c, _):
-            col = pl.multiple_of(c * (8 * COLS), 8 * COLS)
-            acc = conv_block(pg, row, col, True)
-            for i in range(ROWS):
-                at = pl.ds(pl.multiple_of((row + i) * side + col, 8 * COLS), 8 * COLS)
-                wet = mask_ref[at, :].astype(F32)
-                grad = c_ref[at, :].astype(F32)
-                out_ref[at, :] = (wet * (grad + jnp.concatenate(acc[i], 0))).astype(BF16)
-            return 0
-
-        lax.fori_loop(0, col_steps, one, 0)
-        return 0
-
-    marks = [row_steps * n // 4 for n in range(5)]
-    lax.fori_loop(marks[0], marks[1], input_rows, 0)
-
+    for copy in rs_y:
+        copy.wait_recv()
+    y_start = b_start + at_yh * y_rows
+    y_at = pl.ds(pl.multiple_of(y_start, y_rows), y_rows)
+    total[core, y_at, :] = sums[y_piece(at_yh, h)] + (ring_y[0] + ring_y[1] + ring_y[2])
+    y_mate = dev(tile_at((at_yh + 1) % 2, at_z, at_x, core))
+    ag_y = remote(total.at[core, y_at, :], total.at[core, y_at, :], ag_send.at[0], ag_recv.at[0], y_mate)
+    ag_y.start()
+
+    rest = steps * inner_cols
+    lax.fori_loop(0, rest // 2, rest_inner, 0)
+
+    ag_y.wait_recv()
+    ag_b = []
+    for k, b in enumerate(b_peers):
+        block = total.at[core, b_at, :]
+        ag_b.append(remote(block, block, ag_send.at[1 + k], ag_recv.at[1 + k], dev(ring_tile(first, b))))
     for copy in ag_b:
-        copy.wait_recv()
-    ag_a = []
-    for k, a in enumerate(a_peers):
-        block = total.at[core, a_at, :]
-        ag_a.append(remote(block, block, ag_send.at[4 + k], ag_recv.at[4 + k], dev(ring_tile(a, second))))
-    for copy in ag_a:
         copy.start()
 
     sm_core.wait_recv()
@@ -612,34 +644,70 @@
     sm_x = small_stage(
         small_x, small_a[...] + small_core[...], at_x, n_x, 2, lambda x: tile_at(at_yh, at_z, x, core)
     )
-    lax.fori_loop(marks[1], marks[2], input_rows, 0)
-
+    lax.fori_loop(rest // 2, rest, rest_inner, 0)
+
+    for copy in ag_b:
+        copy.wait_recv()
+    ag_a = []
+    for k, a in enumerate(a_peers):
+        block = total.at[core, a_at, :]
+        ag_a.append(remote(block, block, ag_send.at[4 + k], ag_recv.at[4 + k], dev(ring_tile(a, second))))
     for copy in ag_a:
-        copy.wait_recv()
-    ag_core = remote(total.at[core], total.at[core], ag_send.at[7], ag_recv.at[7], core_peer)
-    ag_core.start()
+        copy.start()
 
     for copy in sm_x:
         copy.wait_recv()
     sm_z = small_stage(
         small_z, sum(small_x[k] for k in range(n_x)), at_z, n_z, 5, lambda z: tile_at(at_yh, z, at_x, core)
     )
-    lax.fori_loop(marks[2], marks[3], input_rows, 0)
+    first_halo = row_copies(1)
+    for copy in first_halo:
+        copy.wait_recv()
+    for copy in last_halo:
+        copy.wait_recv()
+    fill_halo(pg, 1)
+    lax.fori_loop(0, row_steps // 2, input_edges, 0)
+
+    for copy in ag_a:
+        copy.wait_recv()
+    ag_core = remote(total.at[core], total.at[core], ag_send.at[7], ag_recv.at[7], core_peer)
+    ag_core.start()
 
     for copy in sm_z:
         copy.wait_recv()
     sm_y = small_stage(
         small_y, sum(small_z[k] for k in range(n_z)), at_yh, 2, 8, lambda yh: tile_at(yh, at_z, at_x, core)
     )
-    mats_ref[core] = total[core] * q
+    lax.fori_loop(row_steps // 2, row_steps, input_edges, 0)
+
+    @pl.when(core == 0)
+    def _():
+        up_sum_ref[...] = total[0] * q
+
+    @pl.when(core == 1)
+    def _():
+        down_sum_ref[...] = total[1].T * q
+
+    for copy in sm_y:
+        copy.wait_recv()
+    small = (small_y[0] + small_y[1]) * q
+    for a in range(KERNEL):
+        taps_ref[a] = small[a * KERNEL : (a + 1) * KERNEL]
+    gain_ref[...] = small[n_taps : n_taps + 1].reshape(LANES)
+    scale_sum_ref[...] = small[n_taps + 1 : n_taps + 2].reshape(LANES)
+    for i in range(4):
+        bias_sum_ref[i * LANES : (i + 1) * LANES] = small[n_taps + 2 + i : n_taps + 3 + i].reshape(LANES)
     ag_core.wait_recv()
-    mats_ref[1 - core] = total[1 - core] * q
-    lax.fori_loop(marks[3], marks[4], input_rows, 0)
-    for copy in sm_y:
-        copy.wait_recv()
-    small_ref[...] = (small_y[0] + small_y[1]) * q
-
-    for copy in weight_copies + forwards + backward_halo + [pars_copy, rs_core, small_chan, sm_core, ag_y, ag_core]:
+
+    @pl.when(core == 1)
+    def _():
+        up_sum_ref[...] = total[0] * q
+
+    @pl.when(core == 0)
+    def _():
+        down_sum_ref[...] = total[1].T * q
+
+    for copy in weight_copies + forwards + first_halo + last_halo + [pars_copy, rs_core, small_chan, sm_core, ag_y, ag_core]:
         copy.wait_send()
     for copy in rs_a + rs_b + rs_y + ag_a + ag_b + sm_x + sm_z + sm_y:
         copy.wait_send()
@@ -648,6 +716,8 @@
         grad_copy(k).wait_send()
         y_copy(k).wait_send()
         conv_copy(k).wait_send()
+        out_copy(k).wait()
+        out_copy(k + steps).wait()
         return 0
 
     lax.fori_loop(0, steps, finish, 0)
@@ -664,17 +734,21 @@
     n_yh, n_z, n_x, n_core = shape4
     width = side + 16
     cells = side * side // 2
-    steps = side // 2 // MLP_ROWS
+    row_steps = side // ROWS
+    steps = row_steps // 2
     a_rows = CHAN // n_x
     vmem = pltpu.VMEM
     whole = pl.BlockSpec(memory_space=pltpu.VMEM)
+    hbm = pl.BlockSpec(memory_space=pl.ANY)
     dma = pltpu.SemaphoreType.DMA
     padded = vmem(((side + 2 * MARGIN) * width, LANES), F32)
     taps = vmem((KERNEL * KERNEL * 8, LANES), F32)
     piece = vmem((cells, LANES), BF16)
     small = vmem((64, LANES), F32)
     pars = vmem((8, HALF_HIDDEN), F32)
+    tile = vmem((side * side, LANES), BF16)
     scratch = [
+        vmem(neighbours.shape, jnp.int32), tile, tile, tile, dma((5,)), dma((row_steps,)),
         padded, padded, taps, taps,
         vmem((4, MARGIN * side, LANES), BF16),
         vmem((2, MARGIN * 16, LANES), BF16),
@@ -684,8 +758,8 @@
         vmem((2, CHAN, HALF_HIDDEN), BF16),
         vmem((2, HALF_HIDDEN, CHAN), BF16),
         pars, pars,
-        vmem((side * side, LANES), BF16), vmem((LANES, LANES), F32),
-        piece, piece, piece, vmem((side * side, LANES), BF16), piece, piece, piece,
+        tile, vmem((LANES, LANES), F32),
+        piece, tile, piece, piece, piece,
         vmem((2, CHAN, HIDDEN), F32),
         vmem((8, CHAN), F32),
         vmem((8, HIDDEN), F32),
@@ -704,11 +778,15 @@
         functools.partial(kernel, side, shape4),
         out_shape=(
             jax.ShapeDtypeStruct(flat, BF16),
-            jax.ShapeDtypeStruct((2, CHAN, HALF_HIDDEN), F32),
-            jax.ShapeDtypeStruct((64, LANES), F32),
+            jax.ShapeDtypeStruct((KERNEL, KERNEL, LANES), F32),
+            jax.ShapeDtypeStruct((LANES,), F32),
+            jax.ShapeDtypeStruct((CHAN, HALF_HIDDEN), F32),
+            jax.ShapeDtypeStruct((HALF_HIDDEN,), F32),
+            jax.ShapeDtypeStruct((HALF_HIDDEN, CHAN), F32),
+            jax.ShapeDtypeStruct((LANES,), F32),
         ),
-        in_specs=[whole] * 10,
-        out_specs=(whole, whole, whole),
+        in_specs=[hbm, hbm, hbm, whole, whole, whole, hbm, whole, hbm, whole],
+        out_specs=(hbm, whole, whole, whole, whole, whole, whole),
         scratch_shapes=scratch,
         compiler_params=pltpu.CompilerParams(
             collective_id=0, has_side_effects=True, vmem_limit_bytes=60 * 1024 * 1024
@@ -719,11 +797,11 @@
         cotangent.reshape(flat),
         wet[0],
         depth_weight,
-        gamma.reshape(1, half_chan),
+        gamma,
         up_weight,
-        up_bias.reshape(1, -1),
+        up_bias,
         down_weight,
-        layer_scale.reshape(1, half_chan),
+        layer_scale,
     )
 
 
@@ -739,19 +817,10 @@
     down_weight,
     layer_scale,
 ):
-    grad, mats, small = block_call(
+    grad, *sums = block_call(
         inputs, cotangent, wet, neighbours, depth_weight, gamma, up_weight, up_bias, down_weight, layer_scale
     )
-    taps = KERNEL * KERNEL
-    return (
-        grad.reshape(inputs.shape),
-        small[:taps].reshape(KERNEL, KERNEL, LANES),
-        small[taps],
-        mats[0],
-        small[taps + 2 : taps + 6].reshape(-1),
-        mats[1].T,
-        small[taps + 1],
-    )
+    return (grad.reshape(inputs.shape), *sums)
 
 
 def solution(mesh):

time: 154 us -> 147 us (0.955)
  Pallas kernels: 141 us -> 136 us
  local copies, waits for them, and re-layouts: 11.1 us -> 8.51 us
    unnamed x5 -> x20, local copies, waits for them, and re-layouts: 3.79 us -> 8.51 us
    pallas_call x1, Pallas kernels: 141 us -> 136 us  [block_call(): pl.pallas_call(functools.partial(kernel, side, shape4), out_shape=(jax.Sh...]
    reshape x3 -> x0, local copies, waits for them, and re-layouts: 3.12 us -> none  [the longest x1 1.26 us: block_call(): up_bias.reshape(1, -1)]
    transpose x1 -> x0, local copies, waits for them, and re-layouts: 2.06 us -> none  [body(): mats[1]]
where the time goes in v3:
time: 147 us; the launch traced here: 146 us
  Pallas kernels  136 us (93%)
  local copies, waits for them, and re-layouts  8.51 us (6%)
    pallas_call x1, Pallas kernels, block_call(): pl.pallas_call(functools.partial(kernel, side, shape4), out_shape=(jax.Sh...  136 us
    unnamed x20, local copies, waits for them, and re-layouts  8.51 us

profile of v3, /device:TPU:1, one launch (start us, length us, event | category | flops | bytes accessed | tf_op | source)
XLA Modules:
  0.0 145.6 jit_solution(8878186934977512614)
XLA Ops:
  0.6 1.4 copy.17.links_in
  2.0 136.4 %shard_map.153 = (bf16[9216,128]{1,0:T(8,128)(2,1)}, f32[7,7,128]{2,1,0:T(8,128)}, f32[128]{0:T(128)}, f32[256,512]{1,0:T(8,128)}, f32[512]{0:T(512)}, /*index=5*/f32[512,256]{1,0:T(8,128)}, f32[128]{0:T(128)}) custom-call(s32[64,8]{1,0:T(8,128)} %copy.17.links_in, bf16[9216,128]{1,0:T(8,128)(2,1)} %bitcast.4, bf16[9216,128]{1,0:T(8,128)(2,1)} %bitcast.5, ...), custom_call_target="tpu_custom_call" | custom-call | tf_op jit(solution)/shard_map/pallas_call | solution.py:777
  138.4 0.0 copy-start.2
  138.4 0.0 copy-start.5
  138.5 0.0 copy-start.1
  138.5 0.0 copy-start.3
  138.5 0.0 copy-start
  138.5 0.0 copy-start.4
  138.5 3.3 %copy.25 = bf16[1,96,96,128]{3,2,1,0:T(8,128)(2,1)} copy(bf16[1,96,96,128]{3,2,1,0:T(8,128)(2,1)} %bitcast.6) | data formatting | bytes 4718592
  141.8 0.0 copy-done.2
  141.8 0.6 copy.26
  142.4 0.0 copy-done.5
  142.4 0.5 copy.27
  142.9 0.0 copy-done.1
  142.9 0.8 copy.28
  143.7 0.0 copy-done.3
  143.7 0.6 copy.29
  144.3 0.0 copy-done
  144.3 0.8 copy.30
  145.1 0.0 copy-done.4
  145.1 0.5 copy.31
Async XLA Ops:
  138.4 3.4 %copy-start.2 = (f32[7,7,128]{2,1,0:T(8,128)S(1)}, f32[7,7,128]{2,1,0:T(8,128)}, u32[]{:S(2)}) copy-start(f32[7,7,128]{2,1,0:T(8,128)} %get-tuple-element.29) | copy-start | bytes 75268
  138.4 4.0 %copy-start.5 = (f32[128]{0:T(128)S(1)}, f32[128]{0:T(128)}, u32[]{:S(2)}) copy-start(f32[128]{0:T(128)} %get-tuple-element.30) | copy-start | bytes 1540
  138.5 4.5 %copy-start.1 = (f32[256,512]{1,0:T(8,128)S(1)}, f32[256,512]{1,0:T(8,128)}, u32[]{:S(2)}) copy-start(f32[256,512]{1,0:T(8,128)} %get-tuple-element.31) | copy-start | bytes 1572868
  138.5 5.3 %copy-start.3 = (f32[512]{0:T(512)S(1)}, f32[512]{0:T(512)}, u32[]{:S(2)}) copy-start(f32[512]{0:T(512)} %get-tuple-element.32) | copy-start | bytes 6148
  138.5 5.8 %copy-start = (f32[512,256]{1,0:T(8,128)S(1)}, f32[512,256]{1,0:T(8,128)}, u32[]{:S(2)}) copy-start(f32[512,256]{1,0:T(8,128)} %get-tuple-element.33) | copy-start | bytes 1572868
  138.5 6.6 %copy-start.4 = (f32[128]{0:T(128)S(1)}, f32[128]{0:T(128)}, u32[]{:S(2)}) copy-start(f32[128]{0:T(128)} %get-tuple-element.34) | copy-start | bytes 1540

commit v4 on v3

--- a/solution.py
+++ b/solution.py
@@ -53,11 +53,11 @@
     side, shape4,
     links_in, x_in, c_in, wet_ref, depth_ref, gamma_ref, up_ref, bias_ref, down_ref, scale_ref,
     out_ref, taps_ref, gain_ref, up_sum_ref, bias_sum_ref, down_sum_ref, scale_sum_ref,
-    links, x_ref, c_ref, out_tile, load_sem, out_sem,
+    links, x_ref, c_ref, load_sem,
     pf, pg, taps, taps_acc, strips, corners, rows_in, cols_in, corners_in,
     wu, wd, pars, pars_in,
     mask_ref, wet_turned, grad_in, y_all, y_in, conv_send, conv_in,
-    sums, gamma_acc, bias_acc, ring_core, ring_a, ring_b, ring_y, total,
+    sums, gamma_acc, bias_acc, core_out, ring_out, ring_core, ring_a, ring_b, ring_y, total,
     small_a, small_peer, small_peer_in, small_core, small_x, small_z, small_y,
     halo_send, halo_recv, weight_sem, weight_recv, grad_sem, grad_recv, y_sem, y_recv, conv_sem, conv_recv,
     rs_send, rs_recv, ag_send, ag_recv, sm_send, sm_recv,
@@ -127,7 +127,6 @@
         pltpu.make_async_copy(c_in, c_ref, load_sem.at[1]),
         pltpu.make_async_copy(up_ref, wu.at[h], load_sem.at[2]),
         pltpu.make_async_copy(down_ref, wd.at[h], load_sem.at[3]),
-        pltpu.make_async_copy(links_in, links, load_sem.at[4]),
     ]
     for copy in loads:
         copy.start()
@@ -135,6 +134,9 @@
     pars[0:1, :] = bias_ref[...].astype(F32).reshape(1, HALF_HIDDEN)
     pars[1:2, 0:LANES] = gamma_ref[...].astype(F32).reshape(1, LANES)
     pars[2:3, 0:LANES] = scale_ref[...].astype(F32).reshape(1, LANES)
+    links[...] = jnp.zeros_like(links)
+    links[0:8, 0:tiles] = links_in[...].astype(F32)
+    links[...] = links[...].T
     wet_turned[...] = jnp.zeros_like(wet_turned)
     wet_turned[0:side, 0:side] = wet_ref[...].astype(F32)
     wet_turned[...] = wet_turned[...].T
@@ -185,8 +187,7 @@
             grad_sem.at[k], grad_recv.at[k], peer,
         )
 
-    for k in range(early):
-        grad_copy(k).start()
+    grad_copy(0).start()
 
     loads[0].wait()
     def fill_input(g, _):
@@ -241,7 +242,7 @@
 
     def match(direction, source):
         link = links[pl.ds(me, 1), direction : direction + 1]
-        return jnp.where(jnp.logical_and(link == source, link >= 0), 1.0, 0.0)
+        return jnp.where(jnp.logical_and(link == lax.convert_element_type(source, F32), link >= 0.0), 1.0, 0.0)
 
     def fill_halo(padded, phase):
         for way, sign in enumerate((-1, 1)):
@@ -276,18 +277,13 @@
     forward_halo = row_copies(0) + col_copies(0)
     for copy in forward_halo:
         copy.start()
-    loads[4].wait()
+    for k in range(1, early):
+        grad_copy(k).start()
 
     for a in range(KERNEL):
         for b in range(KERNEL):
             n = (a * KERNEL + b) * 8
             taps[n : n + 8, :] = jnp.broadcast_to(depth_ref[a, b : b + 1, :], (8, LANES))
-
-    for copy in weight_arrivals:
-        copy.wait_recv()
-    forwards = weight_forward(core)
-    for copy in forwards:
-        copy.start()
 
     def conv_block(padded, row, col, flip):
         base = row * width + col + 8 - MARGIN
@@ -322,6 +318,11 @@
         return 0
 
     lax.fori_loop(0, (row_steps - 2) * (col_steps - 2), conv_inner, 0)
+    for copy in weight_arrivals:
+        copy.wait_recv()
+    forwards = weight_forward(core)
+    for copy in forwards:
+        copy.start()
     for copy in forward_halo:
         copy.wait_recv()
     fill_halo(pf, 0)
@@ -346,9 +347,9 @@
         def _():
             y_copy(n).start()
 
-        @pl.when(n + early < steps)
+        @pl.when(jnp.logical_and(n + 1 >= early, n + 1 < steps))
         def _():
-            grad_copy(n + early).start()
+            grad_copy(n + 1).start()
 
         return 0
 
@@ -462,7 +463,7 @@
             pg[pl.ds(to, side), :] = own[i * side : (i + 1) * side]
         filter_line(line)
 
-        @pl.when(k == steps // 2)
+        @pl.when(k == steps - 2)
         def _():
             take_conv(0)
             row_strips(pg)
@@ -473,7 +474,8 @@
 
     lax.fori_loop(0, steps, mlp, 0)
 
-    rs_core = remote(sums.at[1 - core], ring_core, rs_send.at[0], rs_recv.at[0], core_peer)
+    core_out[...] = sums[1 - core].astype(BF16)
+    rs_core = remote(core_out, ring_core, rs_send.at[0], rs_recv.at[0], core_peer)
     rs_core.start()
 
     ident = lax.broadcasted_iota(jnp.int32, (CHAN, CHAN), 0) == lax.broadcasted_iota(jnp.int32, (CHAN, CHAN), 1)
@@ -512,7 +514,7 @@
             at = pl.ds(pl.multiple_of((row + i) * side + col, 8 * COLS), 8 * COLS)
             wet = mask_ref[at, :].astype(F32)
             grad = c_ref[at, :].astype(F32)
-            out_tile[at, :] = (wet * (grad + jnp.concatenate(acc[i], 0))).astype(BF16)
+            out_ref[at, :] = (wet * (grad + jnp.concatenate(acc[i], 0))).astype(BF16)
 
     inner_cols = col_steps - 2
 
@@ -525,9 +527,6 @@
         input_block(jnp.where(k == 0, line_at(h, steps - 1), line_at(other, k)), 1 + n % inner_cols)
         return 0
 
-    def out_copy(k):
-        return pltpu.make_async_copy(out_tile.at[chunk_rows(k), :], out_ref.at[chunk_rows(k), :], out_sem.at[k])
-
     def input_edges(k, _):
         edge = jnp.logical_or(k == 0, k == row_steps - 1)
 
@@ -536,7 +535,6 @@
             return 0
 
         lax.fori_loop(0, jnp.where(edge, col_steps, 2), one, 0)
-        out_copy(k).start()
         return 0
 
     def peer_line(k, _):
@@ -547,25 +545,28 @@
         filter_line(line_at(other, k))
         return 0
 
-    lax.fori_loop(0, (steps - 2) * inner_cols, own_inner, 0)
+    own = (steps - 2) * inner_cols
+    lax.fori_loop(0, own // 2, own_inner, 0)
+    lax.fori_loop(0, 1, peer_line, 0)
 
     rs_core.wait_recv()
-    sums[core] = sums[core] + ring_core[...]
-    a_rows, b_rows, y_rows = CHAN // n_x, CHAN // n_x // n_z, CHAN // n_x // n_z // 2
+    sums[core] = sums[core] + ring_core[...].astype(F32)
+    ring_out[...] = sums[core].astype(BF16)
+    a_rows, b_rows, y_cols = CHAN // n_x, CHAN // n_x // n_z, HALF_HIDDEN // 2
     rs_a = []
     for k, a in enumerate(a_peers):
-        piece = sums.at[core, pl.ds(pl.multiple_of(a * a_rows, a_rows), a_rows), :]
+        piece = ring_out.at[pl.ds(pl.multiple_of(a * a_rows, a_rows), a_rows), :]
         rs_a.append(remote(piece, ring_a.at[k], rs_send.at[1 + k], rs_recv.at[1 + k], dev(ring_tile(a, second))))
     for copy in rs_a:
         copy.start()
 
-    lax.fori_loop(0, 2, peer_line, 0)
-    lax.fori_loop(2, steps - 2, peer_line, 0)
+    lax.fori_loop(own // 2, own, own_inner, 0)
+    lax.fori_loop(1, steps - 2, peer_line, 0)
 
     for copy in rs_a:
         copy.wait_recv()
     a_at = pl.ds(pl.multiple_of(first * a_rows, a_rows), a_rows)
-    sums[core, a_at, :] = sums[core, a_at, :] + sum(ring_a[k] for k in range(n_x - 1))
+    sums[core, a_at, :] = sums[core, a_at, :] + sum(ring_a[k].astype(F32) for k in range(n_x - 1))
     rs_b = []
     for k, b in enumerate(b_peers):
         piece = sums.at[core, pl.ds(pl.multiple_of(first * a_rows + b * b_rows, b_rows), b_rows), :]
@@ -575,15 +576,24 @@
 
     lax.fori_loop(steps - 2, steps - 1, peer_line, 0)
 
+    take_conv(steps - 1)
+    col_strips(pg)
+    last_halo = col_copies(1)
+    for copy in last_halo:
+        copy.start()
+    filter_line(line_at(other, steps - 1))
+
     for copy in rs_b:
         copy.wait_recv()
     b_start = first * a_rows + second * b_rows
     b_at = pl.ds(pl.multiple_of(b_start, b_rows), b_rows)
     sums[core, b_at, :] = sums[core, b_at, :] + sum(ring_b[k] for k in range(n_x - 1))
 
+    def y_span(yh):
+        return pl.ds(pl.multiple_of(yh * y_cols, y_cols), y_cols)
+
     def y_piece(yh, chan):
-        rows = pl.ds(pl.multiple_of(b_start + yh * y_rows, y_rows), y_rows)
-        return (core, rows, pl.ds(pl.multiple_of(chan * HALF_HIDDEN, HALF_HIDDEN), HALF_HIDDEN))
+        return (core, b_at, pl.ds(pl.multiple_of(chan * HALF_HIDDEN + yh * y_cols, y_cols), y_cols))
 
     rs_y = []
     for k, (dy, dc) in enumerate(y_peers):
@@ -591,13 +601,6 @@
         rs_y.append(remote(piece, ring_y.at[k], rs_send.at[7 + k], rs_recv.at[7 + k], y_dev(dy, dc)))
     for copy in rs_y:
         copy.start()
-
-    take_conv(steps - 1)
-    col_strips(pg)
-    last_halo = col_copies(1)
-    for copy in last_halo:
-        copy.start()
-    filter_line(line_at(other, steps - 1))
 
     for n in range(n_taps):
         small_a[n : n + 1, :] = jnp.sum(taps_acc[n * 8 : n * 8 + 8, :], 0, keepdims=True)
@@ -607,25 +610,16 @@
     sm_core = remote(small_a, small_core, sm_send.at[1], sm_recv.at[1], core_peer)
     sm_core.start()
 
-    for copy in rs_y:
-        copy.wait_recv()
-    y_start = b_start + at_yh * y_rows
-    y_at = pl.ds(pl.multiple_of(y_start, y_rows), y_rows)
-    total[core, y_at, :] = sums[y_piece(at_yh, h)] + (ring_y[0] + ring_y[1] + ring_y[2])
-    y_mate = dev(tile_at((at_yh + 1) % 2, at_z, at_x, core))
-    ag_y = remote(total.at[core, y_at, :], total.at[core, y_at, :], ag_send.at[0], ag_recv.at[0], y_mate)
-    ag_y.start()
-
     rest = steps * inner_cols
     lax.fori_loop(0, rest // 2, rest_inner, 0)
 
-    ag_y.wait_recv()
-    ag_b = []
-    for k, b in enumerate(b_peers):
-        block = total.at[core, b_at, :]
-        ag_b.append(remote(block, block, ag_send.at[1 + k], ag_recv.at[1 + k], dev(ring_tile(first, b))))
-    for copy in ag_b:
-        copy.start()
+    for copy in rs_y:
+        copy.wait_recv()
+    y_block = total.at[core, b_at, y_span(at_yh)]
+    y_block[...] = (sums[y_piece(at_yh, h)] + (ring_y[0] + ring_y[1] + ring_y[2])).astype(BF16)
+    y_mate = dev(tile_at((at_yh + 1) % 2, at_z, at_x, core))
+    ag_y = remote(y_block, y_block, ag_send.at[0], ag_recv.at[0], y_mate)
+    ag_y.start()
 
     sm_core.wait_recv()
 
@@ -646,6 +640,27 @@
     )
     lax.fori_loop(rest // 2, rest, rest_inner, 0)
 
+    ag_y.wait_recv()
+    ag_b = []
+    for k, b in enumerate(b_peers):
+        block = total.at[core, b_at, :]
+        ag_b.append(remote(block, block, ag_send.at[1 + k], ag_recv.at[1 + k], dev(ring_tile(first, b))))
+    for copy in ag_b:
+        copy.start()
+
+    for copy in sm_x:
+        copy.wait_recv()
+    sm_z = small_stage(
+        small_z, sum(small_x[k] for k in range(n_x)), at_z, n_z, 5, lambda z: tile_at(at_yh, z, at_x, core)
+    )
+    first_halo = row_copies(1)
+    for copy in first_halo:
+        copy.wait_recv()
+    for copy in last_halo:
+        copy.wait_recv()
+    fill_halo(pg, 1)
+    lax.fori_loop(0, row_steps // 2, input_edges, 0)
+
     for copy in ag_b:
         copy.wait_recv()
     ag_a = []
@@ -655,24 +670,6 @@
     for copy in ag_a:
         copy.start()
 
-    for copy in sm_x:
-        copy.wait_recv()
-    sm_z = small_stage(
-        small_z, sum(small_x[k] for k in range(n_x)), at_z, n_z, 5, lambda z: tile_at(at_yh, z, at_x, core)
-    )
-    first_halo = row_copies(1)
-    for copy in first_halo:
-        copy.wait_recv()
-    for copy in last_halo:
-        copy.wait_recv()
-    fill_halo(pg, 1)
-    lax.fori_loop(0, row_steps // 2, input_edges, 0)
-
-    for copy in ag_a:
-        copy.wait_recv()
-    ag_core = remote(total.at[core], total.at[core], ag_send.at[7], ag_recv.at[7], core_peer)
-    ag_core.start()
-
     for copy in sm_z:
         copy.wait_recv()
     sm_y = small_stage(
@@ -680,13 +677,18 @@
     )
     lax.fori_loop(row_steps // 2, row_steps, input_edges, 0)
 
+    for copy in ag_a:
+        copy.wait_recv()
+    ag_core = remote(total.at[core], total.at[core], ag_send.at[7], ag_recv.at[7], core_peer)
+    ag_core.start()
+
     @pl.when(core == 0)
     def _():
-        up_sum_ref[...] = total[0] * q
+        up_sum_ref[...] = total[0].astype(F32) * q
 
     @pl.when(core == 1)
     def _():
-        down_sum_ref[...] = total[1].T * q
+        down_sum_ref[...] = total[1].astype(F32).T * q
 
     for copy in sm_y:
         copy.wait_recv()
@@ -701,11 +703,11 @@
 
     @pl.when(core == 1)
     def _():
-        up_sum_ref[...] = total[0] * q
+        up_sum_ref[...] = total[0].astype(F32) * q
 
     @pl.when(core == 0)
     def _():
-        down_sum_ref[...] = total[1].T * q
+        down_sum_ref[...] = total[1].astype(F32).T * q
 
     for copy in weight_copies + forwards + first_halo + last_halo + [pars_copy, rs_core, small_chan, sm_core, ag_y, ag_core]:
         copy.wait_send()
@@ -716,14 +718,33 @@
         grad_copy(k).wait_send()
         y_copy(k).wait_send()
         conv_copy(k).wait_send()
-        out_copy(k).wait()
-        out_copy(k + steps).wait()
         return 0
 
     lax.fori_loop(0, steps, finish, 0)
 
 
 SHAPES = {64: (2, 4, 4, 2), 16: (2, 2, 2, 2)}
+
+
+def hand_over(*refs):
+    count = (len(refs) - 1) // 2
+    sems = refs[-1]
+    copies = [pltpu.make_async_copy(refs[n], refs[count + n], sems.at[n]) for n in range(count)]
+    for copy in copies:
+        copy.start()
+    for copy in copies:
+        copy.wait()
+
+
+def place(results):
+    hbm = pl.BlockSpec(memory_space=pl.ANY)
+    return pl.pallas_call(
+        hand_over,
+        out_shape=tuple(jax.ShapeDtypeStruct(r.shape, r.dtype) for r in results),
+        in_specs=[hbm] * len(results),
+        out_specs=(hbm,) * len(results),
+        scratch_shapes=[pltpu.SemaphoreType.DMA((len(results),))],
+    )(*results)
 
 
 def block_call(inputs, cotangent, wet, neighbours, depth_weight, gamma, up_weight, up_bias, down_weight, layer_scale):
@@ -748,7 +769,7 @@
     pars = vmem((8, HALF_HIDDEN), F32)
     tile = vmem((side * side, LANES), BF16)
     scratch = [
-        vmem(neighbours.shape, jnp.int32), tile, tile, tile, dma((5,)), dma((row_steps,)),
+        vmem((LANES, LANES), F32), tile, tile, dma((4,)),
         padded, padded, taps, taps,
         vmem((4, MARGIN * side, LANES), BF16),
         vmem((2, MARGIN * 16, LANES), BF16),
@@ -763,11 +784,11 @@
         vmem((2, CHAN, HIDDEN), F32),
         vmem((8, CHAN), F32),
         vmem((8, HIDDEN), F32),
-        vmem((CHAN, HIDDEN), F32),
-        vmem((n_x - 1, a_rows, HIDDEN), F32),
+        vmem((CHAN, HIDDEN), BF16), vmem((CHAN, HIDDEN), BF16), vmem((CHAN, HIDDEN), BF16),
+        vmem((n_x - 1, a_rows, HIDDEN), BF16),
         vmem((n_x - 1, a_rows // n_z, HIDDEN), F32),
-        vmem((3, a_rows // n_z // 2, HALF_HIDDEN), F32),
-        vmem((2, CHAN, HALF_HIDDEN), F32),
+        vmem((3, a_rows // n_z, HALF_HIDDEN // 2), F32),
+        vmem((2, CHAN, HALF_HIDDEN), BF16),
         small, vmem((8, LANES), F32), vmem((8, LANES), F32), small,
         vmem((n_x, 64, LANES), F32), vmem((n_z, 64, LANES), F32), vmem((2, 64, LANES), F32),
         dma((2, 12)), dma((2, 12)), dma((7,)), dma((7,)),
@@ -785,14 +806,14 @@
             jax.ShapeDtypeStruct((HALF_HIDDEN, CHAN), F32),
             jax.ShapeDtypeStruct((LANES,), F32),
         ),
-        in_specs=[hbm, hbm, hbm, whole, whole, whole, hbm, whole, hbm, whole],
-        out_specs=(hbm, whole, whole, whole, whole, whole, whole),
+        in_specs=[whole, hbm, hbm, whole, whole, whole, hbm, whole, hbm, whole],
+        out_specs=(whole, whole, whole, whole, whole, whole, whole),
         scratch_shapes=scratch,
         compiler_params=pltpu.CompilerParams(
             collective_id=0, has_side_effects=True, vmem_limit_bytes=60 * 1024 * 1024
         ),
     )(
-        neighbours,
+        neighbours.T,
         inputs.reshape(flat),
         cotangent.reshape(flat),
         wet[0],
@@ -817,9 +838,10 @@
     down_weight,
     layer_scale,
 ):
-    grad, *sums = block_call(
+    results = block_call(
         inputs, cotangent, wet, neighbours, depth_weight, gamma, up_weight, up_bias, down_weight, layer_scale
     )
+    grad, *sums = place(results)
     return (grad.reshape(inputs.shape), *sums)
 
 

time: 147 us -> 231 us (1.57)
  Pallas kernels: 136 us -> 231 us
  local copies, waits for them, and re-layouts: 8.51 us -> 0 us
    pallas_call x0 -> x1, Pallas kernels: none -> 105 us  [place(): pl.pallas_call(hand_over, out_shape=tuple((jax.ShapeDtypeStruct(r.shape,...]
    pallas_call x1, Pallas kernels: 136 us -> 125 us  [block_call(): pl.pallas_call(functools.partial(kernel, side, shape4), out_shape=(jax.Sh...]
    unnamed x20 -> x0, local copies, waits for them, and re-layouts: 8.51 us -> none
where the time goes in v4:
time: 231 us
  Pallas kernels  231 us (100%)
    pallas_call x1, Pallas kernels, block_call(): pl.pallas_call(functools.partial(kernel, side, shape4), out_shape=(jax.Sh...  125 us
    pallas_call x1, Pallas kernels, place(): pl.pallas_call(hand_over, out_shape=tuple((jax.ShapeDtypeStruct(r.shape,...  105 us

profile of v4, /device:TPU:1, one launch (start us, length us, event | category | flops | bytes accessed | tf_op | source)
XLA Modules:
  0.0 231.2 jit_solution(7074343032393039217)
XLA Ops:
  0.6 125.3 %shard_map.153 = (bf16[9216,128]{1,0:T(8,128)(2,1)}, f32[7,7,128]{2,1,0:T(8,128)}, f32[128]{0:T(128)}, f32[256,512]{1,0:T(8,128)}, f32[512]{0:T(512)}, /*index=5*/f32[512,256]{1,0:T(8,128)}, f32[128]{0:T(128)}) custom-call(s32[8,64]{1,0:T(8,128)} %bitcast.8, bf16[9216,128]{1,0:T(8,128)(2,1)} %bitcast.5, bf16[9216,128]{1,0:T(8,128)(2,1)} %bitcast.6, ...), custom_call_target="tpu_custom_call" | custom-call | tf_op jit(solution)/shard_map/pallas_call | solution.py:798
  125.9 105.3 %shard_map.154 = (bf16[9216,128]{1,0:T(8,128)(2,1)}, f32[7,7,128]{2,1,0:T(8,128)}, f32[128]{0:T(128)}, f32[256,512]{1,0:T(8,128)}, f32[512]{0:T(512)}, /*index=5*/f32[512,256]{1,0:T(8,128)}, f32[128]{0:T(128)}) custom-call(bf16[9216,128]{1,0:T(8,128)(2,1)} %get-tuple-element.21.refs_0_, f32[7,7,128]{2,1,0:T(8,128)} %get-tuple-element.22.refs_1_, ...), custom_call_target="tpu_custom_call" | custom-call | tf_op jit(solution)/shard_map/pallas_call | solution.py:741

commit v5 on v4

--- a/solution.py
+++ b/solution.py
@@ -59,7 +59,7 @@
     mask_ref, wet_turned, grad_in, y_all, y_in, conv_send, conv_in,
     sums, gamma_acc, bias_acc, core_out, ring_out, ring_core, ring_a, ring_b, ring_y, total,
     small_a, small_peer, small_peer_in, small_core, small_x, small_z, small_y,
-    halo_send, halo_recv, weight_sem, weight_recv, grad_sem, grad_recv, y_sem, y_recv, conv_sem, conv_recv,
+    halo_send, halo_recv, relay_send, weight_sem, weight_recv, grad_sem, grad_recv, y_sem, y_recv, conv_sem, conv_recv,
     rs_send, rs_recv, ag_send, ag_recv, sm_send, sm_recv,
 ):
     n_yh, n_z, n_x, n_core = shape4
@@ -217,28 +217,94 @@
                 line = padded[pl.ds(MARGIN * width + col + k, side, stride=width), :]
                 strips[2 + side_at, k * side : (k + 1) * side, :] = line.astype(BF16)
 
+    def halo_copy(src, dst, phase, n, sign, d):
+        copy = remote(src, dst, halo_send.at[phase, n], halo_recv.at[phase, n], dev(halo_tile(sign, d)))
+        to, source = me + sign * d, me - sign * d
+        leaves = jnp.logical_and(to >= 0, to < tiles)
+        comes = jnp.logical_and(source >= 0, source < tiles)
+        return copy, dst, leaves, comes
+
+    span = tiles // n_yh
+    farthest = REACH - 1
+    beyond = (me - span, span - 1 - me)
+
+    def hands_on(way, steps_back):
+        return jnp.logical_and(beyond[way] >= steps_back, beyond[way] < farthest)
+
+    def crosses(sign, d):
+        return (me + sign * d + tiles) // span != (me + tiles) // span
+
+    def row_copy(phase, n, sign, d, way):
+        copy, dst, leaves, comes = halo_copy(strips.at[1 - way], rows_in.at[phase, way, d - 1], phase, n, sign, d)
+        if d < farthest:
+            leaves = jnp.logical_and(leaves, jnp.logical_not(crosses(sign, d)))
+        return copy, dst, leaves, comes
+
     def row_copies(phase):
         copies = []
         for n, (sign, d) in enumerate(halo):
-            device = dev(halo_tile(sign, d))
             way = 0 if sign > 0 else 1
-            send = halo_send.at[phase, n]
-            recv = halo_recv.at[phase, n]
             if d < REACH:
-                copies.append(remote(strips.at[1 - way], rows_in.at[phase, way, d - 1], send, recv, device))
+                copies.append(row_copy(phase, n, sign, d, way))
             else:
-                copies.append(remote(corners.at[1 - way], corners_in.at[phase, way], send, recv, device))
+                copies.append(halo_copy(corners.at[1 - way], corners_in.at[phase, way], phase, n, sign, d))
         return copies
 
     def col_copies(phase):
         copies = []
         for way, sign in enumerate((1, -1)):
-            device = dev(halo_tile(sign, 1))
-            n = len(halo) + way
-            copies.append(
-                remote(strips.at[3 - way], cols_in.at[phase, way], halo_send.at[phase, n], halo_recv.at[phase, n], device)
+            copies.append(halo_copy(strips.at[3 - way], cols_in.at[phase, way], phase, len(halo) + way, sign, 1))
+        return copies
+
+    def halo_start(copies):
+        for copy, _, leaves, _ in copies:
+            pl.when(leaves)(copy.start)
+
+    def rows_start(copies, crossing):
+        for (sign, d), (copy, _, leaves, _) in zip(halo, copies):
+            over = crosses(sign, d)
+            pl.when(jnp.logical_and(leaves, over if crossing else jnp.logical_not(over)))(copy.start)
+
+    def relay_copies(phase, way):
+        sign = 1 - 2 * way
+        return [
+            remote(
+                rows_in.at[phase, way, farthest - 1], rows_in.at[phase, way, farthest - i - 1],
+                relay_send.at[phase, i - 1], halo_recv.at[phase, way * REACH + farthest - i - 1],
+                dev(halo_tile(-sign, i)),
             )
-        return copies
+            for i in range(1, farthest)
+        ]
+
+    def relay(phase):
+        for way in range(2):
+
+            @pl.when(hands_on(way, 1))
+            def _(way=way):
+                row_copies(phase)[way * REACH + farthest - 1][0].wait_recv()
+
+            for i, copy in enumerate(relay_copies(phase, way)):
+                pl.when(hands_on(way, i + 1))(copy.start)
+
+    def relay_left(phase):
+        for way in range(2):
+            for i, copy in enumerate(relay_copies(phase, way)):
+                pl.when(hands_on(way, i + 1))(copy.wait_send)
+
+    def halo_arrive(copies):
+        for n, (copy, dst, _, comes) in enumerate(copies):
+            waits = comes
+            if n < len(halo) and n % REACH == farthest - 1:
+                waits = jnp.logical_and(comes, jnp.logical_not(hands_on(n // REACH, 1)))
+            pl.when(waits)(copy.wait_recv)
+
+            @pl.when(jnp.logical_not(comes))
+            def _(dst=dst):
+                dst[...] = jnp.zeros(dst.shape, BF16)
+
+    def halo_left(copies):
+        for copy, _, leaves, _ in copies:
+            pl.when(leaves)(copy.wait_send)
 
     def match(direction, source):
         link = links[pl.ds(me, 1), direction : direction + 1]
@@ -275,8 +341,7 @@
     row_strips(pf)
     col_strips(pf)
     forward_halo = row_copies(0) + col_copies(0)
-    for copy in forward_halo:
-        copy.start()
+    halo_start(forward_halo)
     for k in range(1, early):
         grad_copy(k).start()
 
@@ -317,14 +382,16 @@
         filter_forward(1 + n // (col_steps - 2), 1 + n % (col_steps - 2))
         return 0
 
-    lax.fori_loop(0, (row_steps - 2) * (col_steps - 2), conv_inner, 0)
+    inner = (row_steps - 2) * (col_steps - 2)
+    lax.fori_loop(0, inner // 2, conv_inner, 0)
+    relay(0)
+    lax.fori_loop(inner // 2, inner, conv_inner, 0)
     for copy in weight_arrivals:
         copy.wait_recv()
     forwards = weight_forward(core)
     for copy in forwards:
         copy.start()
-    for copy in forward_halo:
-        copy.wait_recv()
+    halo_arrive(forward_halo)
     fill_halo(pf, 0)
 
     def y_copy(k):
@@ -360,8 +427,7 @@
         copy.wait_recv()
     for copy in loads[1:4]:
         copy.wait()
-    for copy in forward_halo:
-        copy.wait_send()
+    halo_left(forward_halo)
     mine = h == 0
 
     def ordered(own, others):
@@ -467,8 +533,11 @@
         def _():
             take_conv(0)
             row_strips(pg)
-            for copy in row_copies(1):
-                copy.start()
+            rows_start(row_copies(1), False)
+
+        @pl.when(k == steps - 1)
+        def _():
+            rows_start(row_copies(1), True)
 
         return 0
 
@@ -523,8 +592,8 @@
         return 0
 
     def rest_inner(n, _):
-        k = n // inner_cols
-        input_block(jnp.where(k == 0, line_at(h, steps - 1), line_at(other, k)), 1 + n % inner_cols)
+        k = 1 + n // inner_cols
+        input_block(jnp.where(k == steps, line_at(h, steps - 1), line_at(other, k)), 1 + n % inner_cols)
         return 0
 
     def input_edges(k, _):
@@ -574,14 +643,10 @@
     for copy in rs_b:
         copy.start()
 
+    relay(1)
     lax.fori_loop(steps - 2, steps - 1, peer_line, 0)
-
-    take_conv(steps - 1)
-    col_strips(pg)
-    last_halo = col_copies(1)
-    for copy in last_halo:
-        copy.start()
-    filter_line(line_at(other, steps - 1))
+    rest = steps * inner_cols
+    lax.fori_loop(0, rest // 2, rest_inner, 0)
 
     for copy in rs_b:
         copy.wait_recv()
@@ -601,6 +666,12 @@
         rs_y.append(remote(piece, ring_y.at[k], rs_send.at[7 + k], rs_recv.at[7 + k], y_dev(dy, dc)))
     for copy in rs_y:
         copy.start()
+
+    take_conv(steps - 1)
+    col_strips(pg)
+    last_halo = col_copies(1)
+    halo_start(last_halo)
+    filter_line(line_at(other, steps - 1))
 
     for n in range(n_taps):
         small_a[n : n + 1, :] = jnp.sum(taps_acc[n * 8 : n * 8 + 8, :], 0, keepdims=True)
@@ -610,8 +681,7 @@
     sm_core = remote(small_a, small_core, sm_send.at[1], sm_recv.at[1], core_peer)
     sm_core.start()
 
-    rest = steps * inner_cols
-    lax.fori_loop(0, rest // 2, rest_inner, 0)
+    lax.fori_loop(rest // 2, rest, rest_inner, 0)
 
     for copy in rs_y:
         copy.wait_recv()
@@ -638,7 +708,11 @@
     sm_x = small_stage(
         small_x, small_a[...] + small_core[...], at_x, n_x, 2, lambda x: tile_at(at_yh, at_z, x, core)
     )
-    lax.fori_loop(rest // 2, rest, rest_inner, 0)
+    first_halo = row_copies(1)
+    halo_arrive(first_halo + last_halo)
+    fill_halo(pg, 1)
+    marks = [row_steps * n // 4 for n in range(5)]
+    lax.fori_loop(marks[0], marks[1], input_edges, 0)
 
     ag_y.wait_recv()
     ag_b = []
@@ -648,18 +722,14 @@
     for copy in ag_b:
         copy.start()
 
+    lax.fori_loop(marks[1], marks[2], input_edges, 0)
+
     for copy in sm_x:
         copy.wait_recv()
     sm_z = small_stage(
         small_z, sum(small_x[k] for k in range(n_x)), at_z, n_z, 5, lambda z: tile_at(at_yh, z, at_x, core)
     )
-    first_halo = row_copies(1)
-    for copy in first_halo:
-        copy.wait_recv()
-    for copy in last_halo:
-        copy.wait_recv()
-    fill_halo(pg, 1)
-    lax.fori_loop(0, row_steps // 2, input_edges, 0)
+    lax.fori_loop(marks[2], marks[3], input_edges, 0)
 
     for copy in ag_b:
         copy.wait_recv()
@@ -670,13 +740,13 @@
     for copy in ag_a:
         copy.start()
 
+    lax.fori_loop(marks[3], marks[4], input_edges, 0)
+
     for copy in sm_z:
         copy.wait_recv()
     sm_y = small_stage(
         small_y, sum(small_z[k] for k in range(n_z)), at_yh, 2, 8, lambda yh: tile_at(yh, at_z, at_x, core)
     )
-    lax.fori_loop(row_steps // 2, row_steps, input_edges, 0)
-
     for copy in ag_a:
         copy.wait_recv()
     ag_core = remote(total.at[core], total.at[core], ag_send.at[7], ag_recv.at[7], core_peer)
@@ -709,7 +779,10 @@
     def _():
         down_sum_ref[...] = total[1].astype(F32).T * q
 
-    for copy in weight_copies + forwards + first_halo + last_halo + [pars_copy, rs_core, small_chan, sm_core, ag_y, ag_core]:
+    halo_left(first_halo + last_halo)
+    relay_left(0)
+    relay_left(1)
+    for copy in weight_copies + forwards + [pars_copy, rs_core, small_chan, sm_core, ag_y, ag_core]:
         copy.wait_send()
     for copy in rs_a + rs_b + rs_y + ag_a + ag_b + sm_x + sm_z + sm_y:
         copy.wait_send()
@@ -727,23 +800,18 @@
 
 
 def hand_over(*refs):
-    count = (len(refs) - 1) // 2
-    sems = refs[-1]
-    copies = [pltpu.make_async_copy(refs[n], refs[count + n], sems.at[n]) for n in range(count)]
-    for copy in copies:
-        copy.start()
-    for copy in copies:
-        copy.wait()
+    count = len(refs) // 2
+    for source, result in zip(refs[:count], refs[count:]):
+        result[...] = source[...]
 
 
 def place(results):
-    hbm = pl.BlockSpec(memory_space=pl.ANY)
+    whole = pl.BlockSpec(memory_space=pltpu.VMEM)
     return pl.pallas_call(
         hand_over,
         out_shape=tuple(jax.ShapeDtypeStruct(r.shape, r.dtype) for r in results),
-        in_specs=[hbm] * len(results),
-        out_specs=(hbm,) * len(results),
-        scratch_shapes=[pltpu.SemaphoreType.DMA((len(results),))],
+        in_specs=[whole] * len(results),
+        out_specs=(whole,) * len(results),
     )(*results)
 
 
@@ -791,7 +859,7 @@
         vmem((2, CHAN, HALF_HIDDEN), BF16),
         small, vmem((8, LANES), F32), vmem((8, LANES), F32), small,
         vmem((n_x, 64, LANES), F32), vmem((n_z, 64, LANES), F32), vmem((2, 64, LANES), F32),
-        dma((2, 12)), dma((2, 12)), dma((7,)), dma((7,)),
+        dma((2, 12)), dma((2, 12)), dma((2, 3)), dma((7,)), dma((7,)),
         dma((steps,)), dma((steps,)), dma((steps,)), dma((steps,)), dma((steps,)), dma((steps,)),
         dma((10,)), dma((10,)), dma((8,)), dma((8,)), dma((9,)), dma((9,)),
     ]
@@ -838,11 +906,10 @@
     down_weight,
     layer_scale,
 ):
-    results = block_call(
+    grad, *sums = block_call(
         inputs, cotangent, wet, neighbours, depth_weight, gamma, up_weight, up_bias, down_weight, layer_scale
     )
-    grad, *sums = place(results)
-    return (grad.reshape(inputs.shape), *sums)
+    return (grad.reshape(inputs.shape), *place(sums))
 
 
 def solution(mesh):

time: 231 us -> 122 us (0.53)
  Pallas kernels: 231 us -> 118 us
  local copies, waits for them, and re-layouts: 0 us -> 3.22 us
    pallas_call x1, Pallas kernels: 105 us -> 2.24 us  [place(): pl.pallas_call(hand_over, out_shape=tuple((jax.ShapeDtypeStruct(r.shape,...]
    pallas_call x1, Pallas kernels: 125 us -> 116 us  [block_call(): pl.pallas_call(functools.partial(kernel, side, shape4), out_shape=(jax.Sh...]
    unnamed x0 -> x1, local copies, waits for them, and re-layouts: none -> 3.22 us
where the time goes in v5:
time: 122 us
  Pallas kernels  118 us (97%)
  local copies, waits for them, and re-layouts  3.22 us (3%)
    pallas_call x1, Pallas kernels, block_call(): pl.pallas_call(functools.partial(kernel, side, shape4), out_shape=(jax.Sh...  116 us
    unnamed x1, local copies, waits for them, and re-layouts  3.22 us

profile of v5, /device:TPU:1, one launch (start us, length us, event | category | flops | bytes accessed | tf_op | source)
XLA Modules:
  0.0 121.9 jit_solution(4427048171131721224)
XLA Ops:
  0.6 115.8 %shard_map.153 = (bf16[9216,128]{1,0:T(8,128)(2,1)}, f32[7,7,128]{2,1,0:T(8,128)}, f32[128]{0:T(128)}, f32[256,512]{1,0:T(8,128)}, f32[512]{0:T(512)}, /*index=5*/f32[512,256]{1,0:T(8,128)}, f32[128]{0:T(128)}) custom-call(s32[8,64]{1,0:T(8,128)} %bitcast.9, bf16[9216,128]{1,0:T(8,128)(2,1)} %bitcast.5, bf16[9216,128]{1,0:T(8,128)(2,1)} %bitcast.6, ...), custom_call_target="tpu_custom_call" | custom-call | tf_op jit(solution)/shard_map/pallas_call | solution.py:866
  116.5 2.2 %shard_map.154 = (f32[7,7,128]{2,1,0:T(8,128)}, f32[128]{0:T(128)}, f32[256,512]{1,0:T(8,128)}, f32[512]{0:T(512)}, f32[512,256]{1,0:T(8,128)}, /*index=5*/f32[128]{0:T(128)}) custom-call(f32[7,7,128]{2,1,0:T(8,128)} %get-tuple-element.21.refs_0_, f32[128]{0:T(128)} %get-tuple-element.22.refs_1_, f32[256,512]{1,0:T(8,128)} %get-tuple-element.23.refs_2_, ...), custom_call_target="tpu_custom_call" | custom-call | tf_op jit(solution)/shard_map/pallas_call | solution.py:810
  118.7 3.2 %copy.18 = bf16[1,96,96,128]{3,2,1,0:T(8,128)(2,1)} copy(bf16[1,96,96,128]{3,2,1,0:T(8,128)(2,1)} %bitcast.7) | data formatting | bytes 4718592

commit v6 on v5

--- a/solution.py
+++ b/solution.py
@@ -21,24 +21,23 @@
 F32 = jnp.float32
 BF16 = jnp.bfloat16
 MESH = pl.DeviceIdType.MESH
-density = 0.3989422804014327
 half_log2 = -0.7213475204444817
+log2_density = -0.3257480647361593
+rise_fit = (
+    0.7978803240566237, 0.036352056236426934, -5.1744776236202565e-05, -4.809871843393557e-05,
+    2.8097794756336268e-06, -5.43899168917672e-08,
+)
 
 
 def gelu_pieces(hidden):
-    size = jnp.abs(hidden)
-    denom = 1.0 + 0.2316419 * size
-    inverse = pl.reciprocal(denom, approx=True)
-    inverse = inverse * (2.0 - denom * inverse)
-    bell = jnp.exp2(hidden * hidden * half_log2)
-    poly = 0.5 * 1.061405429
-    for factor in (-1.453152027, 1.421413741, -0.284496736, 0.254829592):
-        poly = poly * inverse + 0.5 * factor
-    tail = poly * inverse * bell
-    normal_cdf = jnp.where(hidden >= 0.0, 1.0 - tail, tail)
-    activated = hidden * normal_cdf
-    slope = normal_cdf + hidden * bell * density
-    return activated, slope
+    square = hidden * hidden
+    bounded = jnp.minimum(square, 36.0)
+    poly = rise_fit[-1]
+    for factor in rise_fit[-2::-1]:
+        poly = poly * bounded + factor
+    rise = 1.0 + jnp.tanh(poly * hidden)
+    bell = jnp.exp2(square * half_log2 + log2_density)
+    return hidden * rise, rise + hidden * bell
 
 
 def nn(a, b):
@@ -438,6 +437,7 @@
         return jnp.concatenate(ordered(own, others), 1)
 
     gamma_row = row_of(1)
+    half_gamma = 0.5 * gamma_row
     scale_row = row_of(2)
     bias_rows = ordered(pars[0:1, :], pars_in[0:1, :])
 
@@ -517,7 +517,7 @@
             bias_acc[:, cols] += up_terms[CHAN : CHAN + 8]
             norm_grad = norm_grad + nt(hidden_grad, w_up)
         gamma_acc[...] += jnp.sum((norm_grad * unit).reshape(chunk // 8, 8, CHAN), 0)
-        scaled = norm_grad * gamma_row
+        scaled = norm_grad * half_gamma
         mean = jnp.sum(scaled, 1, keepdims=True) * (1.0 / CHAN)
         tilt = jnp.sum(scaled * unit, 1, keepdims=True) * (1.0 / CHAN)
         conv_grad = (inv_spread * (scaled - mean - unit * tilt)).astype(BF16).astype(F32)
@@ -529,15 +529,13 @@
             pg[pl.ds(to, side), :] = own[i * side : (i + 1) * side]
         filter_line(line)
 
-        @pl.when(k == steps - 2)
+        @pl.when(k == steps - 1)
         def _():
             take_conv(0)
             row_strips(pg)
-            rows_start(row_copies(1), False)
-
-        @pl.when(k == steps - 1)
-        def _():
-            rows_start(row_copies(1), True)
+            rows = row_copies(1)
+            rows_start(rows, False)
+            rows_start(rows, True)
 
         return 0
 
@@ -555,9 +553,9 @@
     for slot in range(2):
         cols = slice(slot * HALF_HIDDEN, (slot + 1) * HALF_HIDDEN)
         paired = paired + nn(down_high[:, cols], wd[slot]) + nn(down_low[:, cols], wd[slot])
-    scale_sum = jnp.sum(jnp.where(ident, paired, 0.0), 0, keepdims=True) / scale_row
-    gamma_sum = jnp.sum(gamma_acc[...], 0, keepdims=True)
-    bias_sum = bias_acc[0:1, :]
+    scale_sum = 0.5 * jnp.sum(jnp.where(ident, paired, 0.0), 0, keepdims=True) / scale_row
+    gamma_sum = 0.5 * jnp.sum(gamma_acc[...], 0, keepdims=True)
+    bias_sum = 0.5 * bias_acc[0:1, :]
     small_peer[...] = jnp.zeros_like(small_peer)
     small_a[...] = jnp.zeros_like(small_a)
     n_taps = KERNEL * KERNEL
@@ -621,7 +619,7 @@
     rs_core.wait_recv()
     sums[core] = sums[core] + ring_core[...].astype(F32)
     ring_out[...] = sums[core].astype(BF16)
-    a_rows, b_rows, y_cols = CHAN // n_x, CHAN // n_x // n_z, HALF_HIDDEN // 2
+    a_rows, b_rows = CHAN // n_x, CHAN // n_x // n_z
     rs_a = []
     for k, a in enumerate(a_peers):
         piece = ring_out.at[pl.ds(pl.multiple_of(a * a_rows, a_rows), a_rows), :]
@@ -654,16 +652,15 @@
     b_at = pl.ds(pl.multiple_of(b_start, b_rows), b_rows)
     sums[core, b_at, :] = sums[core, b_at, :] + sum(ring_b[k] for k in range(n_x - 1))
 
-    def y_span(yh):
-        return pl.ds(pl.multiple_of(yh * y_cols, y_cols), y_cols)
-
-    def y_piece(yh, chan):
-        return (core, b_at, pl.ds(pl.multiple_of(chan * HALF_HIDDEN + yh * y_cols, y_cols), y_cols))
-
+    def y_piece(chan):
+        return (core, b_at, pl.ds(pl.multiple_of(chan * HALF_HIDDEN, HALF_HIDDEN), HALF_HIDDEN))
+
+    y_slot = 2 * at_yh + h
+    ring_y[y_slot] = sums[y_piece(h)]
     rs_y = []
     for k, (dy, dc) in enumerate(y_peers):
-        piece = sums.at[y_piece((at_yh + dy) % 2, (h + dc) % 2)]
-        rs_y.append(remote(piece, ring_y.at[k], rs_send.at[7 + k], rs_recv.at[7 + k], y_dev(dy, dc)))
+        piece = sums.at[y_piece((h + dc) % 2)]
+        rs_y.append(remote(piece, ring_y.at[y_slot], rs_send.at[7 + k], rs_recv.at[7 + k], y_dev(dy, dc)))
     for copy in rs_y:
         copy.start()
 
@@ -681,15 +678,7 @@
     sm_core = remote(small_a, small_core, sm_send.at[1], sm_recv.at[1], core_peer)
     sm_core.start()
 
-    lax.fori_loop(rest // 2, rest, rest_inner, 0)
-
-    for copy in rs_y:
-        copy.wait_recv()
-    y_block = total.at[core, b_at, y_span(at_yh)]
-    y_block[...] = (sums[y_piece(at_yh, h)] + (ring_y[0] + ring_y[1] + ring_y[2])).astype(BF16)
-    y_mate = dev(tile_at((at_yh + 1) % 2, at_z, at_x, core))
-    ag_y = remote(y_block, y_block, ag_send.at[0], ag_recv.at[0], y_mate)
-    ag_y.start()
+    lax.fori_loop(rest // 2, rest * 3 // 4, rest_inner, 0)
 
     sm_core.wait_recv()
 
@@ -708,13 +697,11 @@
     sm_x = small_stage(
         small_x, small_a[...] + small_core[...], at_x, n_x, 2, lambda x: tile_at(at_yh, at_z, x, core)
     )
-    first_halo = row_copies(1)
-    halo_arrive(first_halo + last_halo)
-    fill_halo(pg, 1)
-    marks = [row_steps * n // 4 for n in range(5)]
-    lax.fori_loop(marks[0], marks[1], input_edges, 0)
-
-    ag_y.wait_recv()
+    lax.fori_loop(rest * 3 // 4, rest, rest_inner, 0)
+
+    for copy in rs_y:
+        copy.wait_recv()
+    total[core, b_at, :] = ((ring_y[0] + ring_y[1]) + (ring_y[2] + ring_y[3])).astype(BF16)
     ag_b = []
     for k, b in enumerate(b_peers):
         block = total.at[core, b_at, :]
@@ -722,15 +709,17 @@
     for copy in ag_b:
         copy.start()
 
-    lax.fori_loop(marks[1], marks[2], input_edges, 0)
+    first_halo = row_copies(1)
+    halo_arrive(first_halo + last_halo)
+    fill_halo(pg, 1)
+    marks = [row_steps * n // 4 for n in range(5)]
+    lax.fori_loop(marks[0], marks[1], input_edges, 0)
 
     for copy in sm_x:
         copy.wait_recv()
     sm_z = small_stage(
         small_z, sum(small_x[k] for k in range(n_x)), at_z, n_z, 5, lambda z: tile_at(at_yh, z, at_x, core)
     )
-    lax.fori_loop(marks[2], marks[3], input_edges, 0)
-
     for copy in ag_b:
         copy.wait_recv()
     ag_a = []
@@ -740,7 +729,7 @@
     for copy in ag_a:
         copy.start()
 
-    lax.fori_loop(marks[3], marks[4], input_edges, 0)
+    lax.fori_loop(marks[1], marks[3], input_edges, 0)
 
     for copy in sm_z:
         copy.wait_recv()
@@ -752,13 +741,15 @@
     ag_core = remote(total.at[core], total.at[core], ag_send.at[7], ag_recv.at[7], core_peer)
     ag_core.start()
 
+    lax.fori_loop(marks[3], marks[4], input_edges, 0)
+
     @pl.when(core == 0)
     def _():
-        up_sum_ref[...] = total[0].astype(F32) * q
+        up_sum_ref[...] = total[0].astype(F32) * (0.5 * q)
 
     @pl.when(core == 1)
     def _():
-        down_sum_ref[...] = total[1].astype(F32).T * q
+        down_sum_ref[...] = total[1].astype(F32).T * (0.5 * q)
 
     for copy in sm_y:
         copy.wait_recv()
@@ -773,16 +764,16 @@
 
     @pl.when(core == 1)
     def _():
-        up_sum_ref[...] = total[0].astype(F32) * q
+        up_sum_ref[...] = total[0].astype(F32) * (0.5 * q)
 
     @pl.when(core == 0)
     def _():
-        down_sum_ref[...] = total[1].astype(F32).T * q
+        down_sum_ref[...] = total[1].astype(F32).T * (0.5 * q)
 
     halo_left(first_halo + last_halo)
     relay_left(0)
     relay_left(1)
-    for copy in weight_copies + forwards + [pars_copy, rs_core, small_chan, sm_core, ag_y, ag_core]:
+    for copy in weight_copies + forwards + [pars_copy, rs_core, small_chan, sm_core, ag_core]:
         copy.wait_send()
     for copy in rs_a + rs_b + rs_y + ag_a + ag_b + sm_x + sm_z + sm_y:
         copy.wait_send()
@@ -855,7 +846,7 @@
         vmem((CHAN, HIDDEN), BF16), vmem((CHAN, HIDDEN), BF16), vmem((CHAN, HIDDEN), BF16),
         vmem((n_x - 1, a_rows, HIDDEN), BF16),
         vmem((n_x - 1, a_rows // n_z, HIDDEN), F32),
-        vmem((3, a_rows // n_z, HALF_HIDDEN // 2), F32),
+        vmem((4, a_rows // n_z, HALF_HIDDEN), F32),
         vmem((2, CHAN, HALF_HIDDEN), BF16),
         small, vmem((8, LANES), F32), vmem((8, LANES), F32), small,
         vmem((n_x, 64, LANES), F32), vmem((n_z, 64, LANES), F32), vmem((2, 64, LANES), F32),
@@ -866,7 +857,7 @@
     return pl.pallas_call(
         functools.partial(kernel, side, shape4),
         out_shape=(
-            jax.ShapeDtypeStruct(flat, BF16),
+            vmem(flat, BF16),
             jax.ShapeDtypeStruct((KERNEL, KERNEL, LANES), F32),
             jax.ShapeDtypeStruct((LANES,), F32),
             jax.ShapeDtypeStruct((CHAN, HALF_HIDDEN), F32),
@@ -878,7 +869,7 @@
         out_specs=(whole, whole, whole, whole, whole, whole, whole),
         scratch_shapes=scratch,
         compiler_params=pltpu.CompilerParams(
-            collective_id=0, has_side_effects=True, vmem_limit_bytes=60 * 1024 * 1024
+            collective_id=0, has_side_effects=True, vmem_limit_bytes=58 * 1024 * 1024
         ),
     )(
         neighbours.T,

time: 122 us -> 115 us (0.943)
  Pallas kernels: 118 us -> 113 us
  local copies, waits for them, and re-layouts: 3.22 us -> 1.41 us
    pallas_call x1, Pallas kernels: 116 us -> 111 us  [block_call(): pl.pallas_call(functools.partial(kernel, side, shape4), out_shape=(vmem(f...]
    unnamed x1, local copies, waits for them, and re-layouts: 3.22 us -> 1.41 us
where the time goes in v6:
time: 115 us
  Pallas kernels  113 us (98%)
  local copies, waits for them, and re-layouts  1.41 us (1%)
    pallas_call x1, Pallas kernels, block_call(): pl.pallas_call(functools.partial(kernel, side, shape4), out_shape=(vmem(f...  111 us

profile of v6, /device:TPU:1, one launch (start us, length us, event | category | flops | bytes accessed | tf_op | source)
XLA Modules:
  0.0 115.2 jit_solution(12619092208194947738)
XLA Ops:
  0.6 110.9 %shard_map.153 = (bf16[9216,128]{1,0:T(8,128)(2,1)S(1)}, f32[7,7,128]{2,1,0:T(8,128)}, f32[128]{0:T(128)}, f32[256,512]{1,0:T(8,128)}, f32[512]{0:T(512)}, /*index=5*/f32[512,256]{1,0:T(8,128)}, f32[128]{0:T(128)}) custom-call(s32[8,64]{1,0:T(8,128)} %bitcast.9, bf16[9216,128]{1,0:T(8,128)(2,1)} %bitcast.6, bf16[9216,128]{1,0:T(8,128)(2,1)} %bitcast.7, ...), custom_call_target="tpu_custom_call" | custom-call | tf_op jit(solution)/shard_map/pallas_call | solution.py:857
  111.5 1.4 %copy.18 = bf16[1,96,96,128]{3,2,1,0:T(8,128)(2,1)} copy(bf16[1,96,96,128]{3,2,1,0:T(8,128)(2,1)S(1)} %bitcast.5) | data formatting | bytes 4718592
  112.9 2.2 %shard_map.154 = (f32[7,7,128]{2,1,0:T(8,128)}, f32[128]{0:T(128)}, f32[256,512]{1,0:T(8,128)}, f32[512]{0:T(512)}, f32[512,256]{1,0:T(8,128)}, /*index=5*/f32[128]{0:T(128)}) custom-call(f32[7,7,128]{2,1,0:T(8,128)} %get-tuple-element.21.refs_0_, f32[128]{0:T(128)} %get-tuple-element.22.refs_1_, f32[256,512]{1,0:T(8,128)} %get-tuple-element.23.refs_2_, ...), custom_call_target="tpu_custom_call" | custom-call | tf_op jit(solution)/shard_map/pallas_call | solution.py:801

commit v7 on v6

--- a/solution.py
+++ b/solution.py
@@ -803,7 +803,7 @@
         out_shape=tuple(jax.ShapeDtypeStruct(r.shape, r.dtype) for r in results),
         in_specs=[whole] * len(results),
         out_specs=(whole,) * len(results),
-    )(*results)
+    )(*(pltpu.with_memory_space_constraint(r, pltpu.VMEM) for r in results))
 
 
 def block_call(inputs, cotangent, wet, neighbours, depth_weight, gamma, up_weight, up_bias, down_weight, layer_scale):
@@ -858,12 +858,12 @@
         functools.partial(kernel, side, shape4),
         out_shape=(
             vmem(flat, BF16),
-            jax.ShapeDtypeStruct((KERNEL, KERNEL, LANES), F32),
-            jax.ShapeDtypeStruct((LANES,), F32),
-            jax.ShapeDtypeStruct((CHAN, HALF_HIDDEN), F32),
-            jax.ShapeDtypeStruct((HALF_HIDDEN,), F32),
-            jax.ShapeDtypeStruct((HALF_HIDDEN, CHAN), F32),
-            jax.ShapeDtypeStruct((LANES,), F32),
+            vmem((KERNEL, KERNEL, LANES), F32),
+            vmem((LANES,), F32),
+            vmem((CHAN, HALF_HIDDEN), F32),
+            vmem((HALF_HIDDEN,), F32),
+            vmem((HALF_HIDDEN, CHAN), F32),
+            vmem((LANES,), F32),
         ),
         in_specs=[whole, hbm, hbm, whole, whole, whole, hbm, whole, hbm, whole],
         out_specs=(whole, whole, whole, whole, whole, whole, whole),

time: 115 us -> 113 us (0.983)
  Pallas kernels: 113 us -> 111 us
    pallas_call x1, Pallas kernels: 2.24 us -> 1.05 us  [place(): pl.pallas_call(hand_over, out_shape=tuple((jax.ShapeDtypeStruct(r.shape,...]
where the time goes in v7:
time: 113 us
  Pallas kernels  111 us (98%)
  local copies, waits for them, and re-layouts  1.41 us (1%)
    pallas_call x1, Pallas kernels, block_call(): pl.pallas_call(functools.partial(kernel, side, shape4), out_shape=(vmem(f...  110 us

profile of v7, /device:TPU:1, one launch (start us, length us, event | category | flops | bytes accessed | tf_op | source)
XLA Modules:
  0.0 113.0 jit_solution(16106457219017088838)
XLA Ops:
  0.6 109.9 %shard_map.153 = (bf16[9216,128]{1,0:T(8,128)(2,1)S(1)}, f32[7,7,128]{2,1,0:T(8,128)S(1)}, f32[128]{0:T(128)S(1)}, f32[256,512]{1,0:T(8,128)S(1)}, f32[512]{0:T(...) custom-call(s32[8,64]{1,0:T(8,128)} %bitcast.9, bf16[9216,128]{1,0:T(8,128)(2,1)} %bitcast.6, ...), custom_call_target="tpu_custom_call" | custom-call | tf_op jit(solution)/shard_map/pallas_call | solution.py:857
  110.5 1.4 %copy.18 = bf16[1,96,96,128]{3,2,1,0:T(8,128)(2,1)} copy(bf16[1,96,96,128]{3,2,1,0:T(8,128)(2,1)S(1)} %bitcast.5) | data formatting | bytes 4718592
  111.9 1.0 shard_map.154
